TPU v7x, 32 devices: a whole 2x2x4 slice. The times are simulated.
32 devices in a mesh: dp: 8 (over z, x), seq: 4 (over y, core).
Axes of the slice: x: 2, y: 2, z: 4, core: 2. Of those that a mesh axis runs over, the one named last changes fastest.
Arguments:
- inputs: bfloat16 [4, 8, 2048, 384], P(None, 'dp', 'seq'), may hold values from -6 to 6
- cotangent: bfloat16 [4, 8, 2048, 384], P(None, 'dp', 'seq'), may hold values from -6 to 6
- counts: int32 [8], P('dp'), may hold values from 2 to 4
- lead_steps: int32 [8, 4], P('dp'), may hold values from 0 to 15
- emb_table: bfloat16 [16, 384], replicated, may hold values from -6 to 6
- w_ada: bfloat16 [384, 2304], replicated, may hold values from -0.3125 to 0.3125
- b_ada: bfloat16 [2304], replicated, may hold values from -3 to 3
- w_qkv: bfloat16 [384, 1152], replicated, may hold values from -0.3125 to 0.3125
- w_out: bfloat16 [384, 384], replicated, may hold values from -1.25 to 1.25
- w_fc1: bfloat16 [384, 1536], replicated, may hold values from -0.3125 to 0.3125
- w_fc2: bfloat16 [1536, 384], replicated, may hold values from -0.15625 to 0.15625
Outputs:
- outputs: bfloat16 [4, 8, 2048, 384], P(None, 'dp', 'seq')
- grad_inputs: bfloat16 [4, 8, 2048, 384], P(None, 'dp', 'seq')
- grad_emb: float32 [16, 384], replicated
- grad_ada: float32 [384, 2304], replicated
- grad_bada: float32 [2304], replicated
- grad_qkv: float32 [384, 1152], replicated
- grad_out: float32 [384, 384], replicated
- grad_fc1: float32 [384, 1536], replicated
- grad_fc2: float32 [1536, 384], replicated
Inputs may be any that keep to these rules, and one draw needn't show every extreme that they name: The step s of item i takes part when s < counts[i].
All inputs are finite; a program needn't handle non-finite values.
Results may differ from a plain program's by a relative error of at most 0.015.
The roundings to bfloat16 on the way count: a program that leaves them out, or rounds other values in their place, can miss the bound.
Values may be sent and summed in bfloat16 or wider, within the bound.
A program may use at most 256 MiB of HBM per device.

v0:
```python
import functools

import jax
import jax.numpy as jnp
from jax import lax
from jax.experimental import pallas as pl
from jax.experimental.pallas import tpu as pltpu
from jax.sharding import PartitionSpec as P

HD = 64
LANES = 128
EPSILON = 1e-06
LOG2E = 1.4426950408889634
NN = (((1,), (0,)), ((), ()))
NT = (((1,), (1,)), ((), ()))
TN = (((0,), (0,)), ((), ()))
F32 = jnp.float32
BF16 = jnp.bfloat16
VMEM_BYTES = 24 * 1024 * 1024


def dot(a, b, dims=NN):
    return lax.dot_general(a, b, dims, preferred_element_type=F32)


def call(
    body,
    name,
    grid,
    in_specs,
    out_specs,
    out_shape,
    scratch=(),
    flops=0,
    moved=0,
    exps=0,
    collective=None,
    aliases=None,
):
    return pl.pallas_call(
        body,
        name=name,
        grid=grid,
        in_specs=in_specs,
        out_specs=out_specs,
        out_shape=out_shape,
        scratch_shapes=list(scratch),
        input_output_aliases=aliases or {},
        cost_estimate=pl.CostEstimate(flops=flops, bytes_accessed=moved, transcendentals=exps),
        compiler_params=pltpu.CompilerParams(
            vmem_limit_bytes=VMEM_BYTES,
            collective_id=collective,
            has_side_effects=collective is not None,
        ),
    )


def whole(shape):
    return pl.BlockSpec(shape, lambda *_: (0,) * len(shape))


def scalars():
    return pl.BlockSpec(memory_space=pltpu.SMEM)


def lane_index(shape):
    return lax.broadcasted_iota(jnp.int32, shape, 1)


def first_step(steps):
    return lax.rem(lax.axis_index("seq"), 2) * steps


def normalize(values):
    center = values - jnp.mean(values, axis=-1, keepdims=True)
    spread = jnp.mean(center * center, axis=-1, keepdims=True)
    inverse = lax.rsqrt(spread + EPSILON)
    return center * inverse, inverse


def norm_back(grad, xhat, inverse):
    first = jnp.mean(grad, axis=-1, keepdims=True)
    second = jnp.mean(grad * xhat, axis=-1, keepdims=True)
    return inverse * (grad - first - xhat * second)


def pick(refs, which):
    value = refs[0][0]
    for index in range(1, len(refs)):
        value = jnp.where(which == index, refs[index][0], value)
    return value


class Exchange:
    def __init__(self, mesh_shape, row_tiles, turn=0):
        bits = {"seq": [], "dp": []}
        for axis in bits:
            bit = 1
            while bit < mesh_shape[axis]:
                bits[axis].append((axis, bit))
                bit *= 2
        turned = bits["dp"][turn:] + bits["dp"][:turn]
        self.bits = bits["seq"][:1] + turned + bits["seq"][1:]
        self.all_levels = len(self.bits)
        self.levels = 1 + len(turned)
        self.even = 0
        while self.even < self.levels and row_tiles % 2 == 0:
            row_tiles //= 2
            self.even += 1
        unit = 2 ** (self.levels - self.even)
        self.groups = 2**self.even
        self.real = row_tiles * 16
        self.padded = -(-row_tiles // unit) * unit * 16
        self.shard = self.padded // unit

    def sizes(self, level):
        if level < self.even:
            return (self.groups >> (level + 1), self.real)
        return (1, self.padded >> (level - self.even + 1))

    def receive_scratch(self, width):
        last = self.levels - 1
        return [
            pltpu.VMEM(self.sizes(min(level, last)) + (width,), BF16)
            for level in range(self.all_levels)
        ]

    def place(self, level):
        axis, bit = self.bits[level]
        here = lax.axis_index(axis)
        value = (here // bit) % 2
        return value, {axis: here + bit * (1 - 2 * value)}

    def spot(self, level, first, flip):
        group, row = 0, 0
        for index in range(first, level + 1):
            value, _ = self.place(index)
            if flip and index == level:
                value = 1 - value
            if index < self.even:
                group = group + value * (self.groups >> (index + 1))
            else:
                row = row + value * (self.padded >> (index - self.even + 1))
        if level >= self.even:
            row = pl.multiple_of(row, 16)
        count, rows = self.sizes(level)
        return pl.ds(group, count), pl.ds(row, rows)

    def barrier(self):
        semaphore = pltpu.get_barrier_semaphore()
        for level in range(self.all_levels):
            _, partner = self.place(level)
            pl.semaphore_signal(
                semaphore, inc=1, device_id=partner, device_id_type=pl.DeviceIdType.MESH
            )
        pl.semaphore_wait(semaphore, self.all_levels)

    def copy(self, source, target, sends, recvs, level):
        _, partner = self.place(level)
        return pltpu.make_async_remote_copy(
            src_ref=source,
            dst_ref=target,
            send_sem=sends.at[level],
            recv_sem=recvs.at[level],
            device_id=partner,
            device_id_type=pl.DeviceIdType.MESH,
        )

    def reduce_copy(self, level, start_ref, acc_ref, got, sends, recvs):
        if level >= self.levels:
            return self.copy(self.own_shard(acc_ref, 1), got[level], sends, recvs, level)
        groups, rows = self.spot(level, min(level, 1), True)
        source = start_ref if level == 0 else acc_ref
        return self.copy(source.at[groups, rows], got[level], sends, recvs, level)

    def reduce_start(self, level, *refs):
        self.reduce_copy(level, *refs).start()

    def reduce_finish(self, level, start_ref, acc_ref, got, sends, recvs):
        self.reduce_copy(level, start_ref, acc_ref, got, sends, recvs).wait()
        if level >= self.levels:
            own = self.own_shard(acc_ref, 1)
            own[...] = (own[...].astype(F32) + got[level][...].astype(F32)).astype(BF16)
            return
        count, rows = self.sizes(level)
        groups, spots = self.spot(level, min(level, 1), False)
        if level == 0:
            target_groups, target_rows = pl.ds(0, count), pl.ds(0, rows)
            if self.padded > self.real:
                acc_ref[:, self.real :, :] = jnp.zeros_like(acc_ref[:, self.real :, :])
        else:
            target_groups, target_rows = groups, spots
        source = start_ref if level == 0 else acc_ref

        def add(index, carry):
            one = pl.ds(groups.start + index, 1)
            to = pl.ds(target_groups.start + index, 1)
            value = source[one, spots, :].astype(F32) + got[level][pl.ds(index, 1)].astype(F32)
            acc_ref[to, target_rows, :] = value.astype(BF16)
            return carry

        lax.fori_loop(0, count, add, 0)

    def own_shard(self, ref, first):
        if self.levels > self.even:
            return ref.at[self.spot(self.levels - 1, first, False)]
        groups, _ = self.spot(self.levels - 1, first, False)
        return ref.at[groups, pl.ds(0, self.shard)]

    def gather_copy(self, level, full_ref, sends, recvs):
        piece = full_ref.at[self.spot(level, 0, False)]
        return self.copy(piece, piece, sends, recvs, level)

    def gather_start(self, level, *refs):
        self.gather_copy(level, *refs).start()

    def gather_finish(self, level, *refs):
        self.gather_copy(level, *refs).wait()


def modulation(lead_ref, emb_ref, ada_ref, bias_ref):
    shape = (16, emb_ref.shape[0])
    rows = lax.broadcasted_iota(jnp.int32, shape, 0)
    columns = lane_index(shape)
    onehot = jnp.zeros(shape, F32)
    for step in range(2):
        lead = lead_ref[0, first_step(2) + step]
        onehot = jnp.where((rows == step) & (columns == lead), 1.0, onehot)
    condition = dot(onehot.astype(BF16), emb_ref[...])
    active = (condition * jax.nn.sigmoid(condition)).astype(BF16)
    return dot(active, ada_ref[...]) + bias_ref[...].astype(F32)


def project(x_refs, mod_ref, step, w_ref, normed_ref, head_refs):
    width = w_ref.shape[0]
    patches = x_refs[0].shape[1]
    rows = min(256, patches)
    shift = mod_ref[pl.ds(step, 1), 0:width]
    scale = mod_ref[pl.ds(step, 1), width : 2 * width]
    queries = len(head_refs) == 3
    for index, x_ref in enumerate(x_refs):

        def block(count, carry):
            start = pl.multiple_of(count * rows, rows)
            at = pl.ds(pl.multiple_of(index * patches + start, rows), rows)
            xhat, _ = normalize(x_ref[0, pl.ds(start, rows), :].astype(F32))
            normed = (xhat * (1.0 + scale) + shift).astype(BF16)
            normed_ref[0, at, :] = normed
            for part, head_ref in enumerate(head_refs):
                first = (part + (0 if queries else 1)) * width
                projected = dot(normed, w_ref[:, first : first + width])
                if queries and part == 0:
                    projected = projected.astype(BF16).astype(F32) * HD**-0.5
                projected = projected.astype(BF16)
                for pair in range(width // LANES):
                    head_ref[0, pair, at, :] = projected[:, pair * LANES : (pair + 1) * LANES]
            return carry

        lax.fori_loop(0, patches // rows, block, 0, unroll=True)


def with_ones(values):
    low = lane_index(values.shape) < HD
    one = jnp.ones_like(values)
    return jnp.where(low, values, one), jnp.where(low, one, values)


def exponentials(query, keys_ref, pair, width=256):
    count = keys_ref.shape[2]
    width = min(width, count)
    return jnp.concatenate(
        [
            jnp.exp(dot(query, keys_ref[0, pair, start : start + width, :], NT)).astype(BF16)
            for start in range(0, count, width)
        ],
        axis=-1,
    )


def masked(values):
    low = lane_index(values.shape) < HD
    zero = jnp.zeros_like(values)
    return jnp.where(low, values, zero), jnp.where(low, zero, values)


def near_kernel(rows, *refs):
    lead_ref, emb_ref, ada_ref, bias_ref, own_x, sib_x, w_ref = refs[:7]
    mod_ref, normed_ref, q_ref, k_ref, v_ref, acc_ref, ext_ref = refs[7:]
    step, pair = pl.program_id(0), pl.program_id(1)

    @pl.when((step == 0) & (pair == 0))
    def _():
        mod_ref[...] = modulation(lead_ref, emb_ref, ada_ref, bias_ref)

    @pl.when(pair == 0)
    def _():
        project([own_x, sib_x], mod_ref, step, w_ref, normed_ref, [q_ref, k_ref, v_ref])

    ext_ref[0], ext_ref[1] = with_ones(v_ref[0, pair])
    for start in range(0, q_ref.shape[2], rows):
        at = slice(start, start + rows)
        for head, query in enumerate(masked(q_ref[0, pair, at, :])):
            acc_ref[0, 0, head, at, :] = dot(exponentials(query, k_ref, pair), ext_ref[head])


def far_kernel(rows, step, sources, *refs):
    x_refs, refs = refs[:sources], refs[sources:]
    mod_ref, w_ref, q_ref, k_ref, v_ref, acc_ref = refs[:6]
    normed_ref, kr_ref, vr_ref, o_ref, qe_ref, ext_ref, total_ref = refs[-7:]
    pair = pl.program_id(0)

    @pl.when(pair == 0)
    def _():
        project(x_refs, mod_ref, step, w_ref, normed_ref, [kr_ref, vr_ref])

    ext_ref[0], ext_ref[1] = with_ones(vr_ref[0, pair])
    def finish(at, query, first, second, top_first, top_second):
        lane = lane_index(query.shape)
        low = lane < HD
        swapped = jnp.where(low, second, first)
        total = pltpu.roll(swapped, HD, 1)
        o_ref[0, 0, at, :] = jnp.where(low, first, second) / total
        log_total = jnp.log(swapped) + jnp.where(low, top_second, top_first)
        high = log_total.astype(BF16).astype(F32)
        middle = (log_total - high).astype(BF16).astype(F32)
        rest = log_total - high - middle
        spot = lane % HD
        extra = jnp.where(spot == 0, -high, jnp.where(spot == 1, -middle, -rest))
        extra = jnp.where(spot < 3, extra, 0.0).astype(BF16)
        qe_ref[0, 0, 0, at, :] = jnp.where(low, query, extra)
        qe_ref[0, 0, 1, at, :] = jnp.where(low, extra, query)
        return total

    def block(index, carry):
        at = pl.ds(pl.multiple_of(index * rows, rows), rows)
        query = q_ref[0, 0, at, :]
        sums = []
        for head, own in enumerate(masked(query)):
            more = dot(exponentials(own, kr_ref, pair), ext_ref[head])
            sums.append(acc_ref[0, 0, head, at, :] + more)
        total_ref[at, :] = finish(at, query, sums[0], sums[1], 0.0, 0.0)
        return carry

    lax.fori_loop(0, q_ref.shape[2] // rows, block, 0, unroll=True)
    total = total_ref[...]
    bad = jnp.sum(jnp.where((total > 1e-25) & (total < 1e25), 0.0, 1.0))

    @pl.when(bad > 0.0)
    def _():
        own_ext = with_ones(v_ref[0, 0])

        again_rows = min(32, q_ref.shape[2])

        def again(index, carry):
            at = pl.ds(pl.multiple_of(index * again_rows, again_rows), again_rows)
            query = q_ref[0, 0, at, :]
            sums, tops = [], []
            for head, own in enumerate(masked(query)):
                scores = dot(own, k_ref[0, 0], NT)
                others = dot(own, kr_ref[0, pair], NT)
                top = jnp.maximum(
                    jnp.max(scores, axis=-1, keepdims=True),
                    jnp.max(others, axis=-1, keepdims=True),
                )
                sums.append(
                    dot(jnp.exp(scores - top).astype(BF16), own_ext[head])
                    + dot(jnp.exp(others - top).astype(BF16), ext_ref[head])
                )
                tops.append(top)
            finish(at, query, sums[0], sums[1], tops[0], tops[1])
            return carry

        lax.fori_loop(0, q_ref.shape[2] // again_rows, again, 0)


def gelu_parts(values):
    cumulative = 0.5 * lax.erf(values * 0.7071067811865476) + 0.5
    bell = jnp.exp2(values * values * (-0.5 * LOG2E))
    return values * cumulative, cumulative + values * bell * 0.3989422804014327


def patch_kernel(
    rows,
    chunk,
    counts_ref,
    lead_ref,
    own_x,
    sib_x,
    own_ct,
    sib_ct,
    mod_ref,
    o_ref,
    out_w,
    fc1_w,
    fc2_w,
    final_own,
    final_sib,
    gm_ref,
    ge_ref,
    sums_ref,
    stack_one,
    stack_two,
    hidden_s,
    gpre_s,
    n2_s,
    g2_s,
    g1_s,
    mixed_s,
    gout_s,
    gfc1_s,
    gfc2_s,
    sums_s,
):
    step, half = pl.program_id(0), pl.program_id(1)
    width, hidden_width = fc1_w.shape
    patches = own_x.shape[1]
    slot = first_step(pl.num_programs(0)) + step
    active = (slot < counts_ref[0]).astype(F32)

    def piece(index):
        return mod_ref[pl.ds(step, 1), index * width : (index + 1) * width]

    gate1, shift2, scale2, gate2 = piece(2), piece(3), piece(4), piece(5)

    @pl.when((step == 0) & (half == 0))
    def _():
        sums_s[...] = jnp.zeros_like(sums_s)
        gout_s[...] = jnp.zeros_like(gout_s)
        gfc1_s[...] = jnp.zeros_like(gfc1_s)
        gfc2_s[...] = jnp.zeros_like(gfc2_s)

    def block(index, carry):
        at = pl.ds(pl.multiple_of(index * rows, rows), rows)
        x = jnp.where(half == 0, own_x[0, at, :], sib_x[0, at, :]).astype(F32)
        final_grad = jnp.where(half == 0, own_ct[0, at, :], sib_ct[0, at, :]).astype(F32) * active
        outs = [o_ref[0, pair, at, :] for pair in range(width // LANES)]
        mixed = jnp.concatenate([o.astype(BF16) for o in outs], axis=-1)
        mixed_s[at, :] = mixed
        branch_one = dot(mixed, out_w[...])
        middle = x + gate1 * branch_one
        xhat, inverse = normalize(middle)
        n2 = (xhat * (1.0 + scale2) + shift2).astype(BF16)
        n2_s[at, :] = n2
        g2 = (gate2 * final_grad).astype(BF16)
        g2_s[at, :] = g2
        branch_two = jnp.zeros((rows, width), F32)
        gy = jnp.zeros((rows, width), F32)
        for start in range(0, hidden_width, chunk):
            columns = slice(start, start + chunk)
            pre = dot(n2, fc1_w[:, columns])
            grad_hidden = dot(g2, fc2_w[columns, :], NT)
            hidden, slope = gelu_parts(pre)
            hidden = hidden.astype(BF16)
            grad_pre = (slope * grad_hidden).astype(BF16)
            hidden_s[at, columns] = hidden
            gpre_s[at, columns] = grad_pre
            branch_two += dot(hidden, fc2_w[columns, :])
            gy += dot(grad_pre, fc1_w[:, columns], NT)
        final = ((middle + gate2 * branch_two) * active).astype(BF16)

        @pl.when(half == 0)
        def _():
            final_own[0, at, :] = final

        @pl.when(half == 1)
        def _():
            final_sib[0, at, :] = final

        gm = final_grad + norm_back(gy * (1.0 + scale2), xhat, inverse)
        gm_ref[0, 0, at, :] = gm
        g1 = (gate1 * gm).astype(BF16)
        g1_s[at, :] = g1
        sums = [branch_one * gm, gy, gy * xhat, branch_two * final_grad]
        for row, value in enumerate(sums):
            place = pl.ds(2 * row + step, 1)
            sums_s[place, :] += jnp.sum(value, axis=0, keepdims=True)
        grad_mixed = dot(g1, out_w[...], NT).astype(BF16)
        lane = lane_index((rows, LANES))
        low = lane < HD
        spot = lane % HD
        for pair, o in enumerate(outs):
            grad = grad_mixed[:, pair * LANES : (pair + 1) * LANES]
            product = grad.astype(F32) * o
            first = jnp.sum(jnp.where(low, product, 0.0), axis=-1, keepdims=True)
            second = jnp.sum(jnp.where(low, 0.0, product), axis=-1, keepdims=True)
            inner = jnp.where(low, second, first)
            high = inner.astype(BF16).astype(F32)
            mid = (inner - high).astype(BF16).astype(F32)
            extra = jnp.where(spot == 0, -high, jnp.where(spot == 1, -mid, high + mid - inner))
            extra = jnp.where(spot < 3, extra, 0.0).astype(BF16)
            ge_ref[0, pair, 0, at, :] = jnp.where(low, grad, extra)
            ge_ref[0, pair, 1, at, :] = jnp.where(low, extra, grad)
        return carry

    lax.fori_loop(0, patches // rows, block, 0)
    gout_s[...] += dot(mixed_s[...], g1_s[...], TN)
    gfc1_s[...] += dot(n2_s[...], gpre_s[...], TN)
    gfc2_s[...] += dot(g2_s[...], hidden_s[...], TN)

    @pl.when((step == pl.num_programs(0) - 1) & (half == pl.num_programs(1) - 1))
    def _():
        for index in range(2):
            lead = lead_ref[0, first_step(2) + index]
            sums_s[12 + index : 13 + index, :] = jnp.where(lane_index((1, width)) == lead, 1.0, 0.0)
        sums_ref[...] = sums_s[...].astype(BF16)
        blocks = hidden_width // width
        for index in range(blocks):
            columns = slice(index * width, (index + 1) * width)
            stack_one[index] = gfc1_s[:, columns].astype(BF16)
            stack_two[index] = gfc2_s[:, columns].T.astype(BF16)
        stack_two[blocks] = gout_s[...].astype(BF16)


def attend_back_kernel(rows, first_pass, exchanges, grid_steps, *refs):
    count = len(exchanges)
    qe_ref, ge_ref, k_ref, v_ref = refs[:4]
    refs = refs[4:]
    if first_pass:
        gives, sums_ref, refs = refs[:count], refs[count], refs[count + 1 :]
        dq_ref, dk_ref, dv_ref = refs[:3]
        shards, all_ref, refs = refs[3 : 3 + count], refs[3 + count], refs[4 + count :]
        all_s, all_sends, all_recvs = refs[-3:]
    else:
        dq_in, shards, refs = refs[0], refs[1 : 1 + count], refs[1 + count :]
        dq_ref, dk_ref, dv_ref = refs[:3]
        fulls, refs = refs[3 : 3 + count], refs[3 + count :]
    dq_s, refs = refs[0], refs[1:]
    states = []
    for index, exchange in enumerate(exchanges):
        sends, recvs = refs[1], refs[2]
        if first_pass:
            got = refs[3 : 3 + exchange.all_levels]
            states.append((gives[index], refs[0], got, sends, recvs))
            refs = refs[3 + exchange.all_levels :]
        else:
            states.append((refs[0], sends, recvs))
            refs = refs[3:]
    per_step = k_ref.shape[2] // rows
    static_slots = grid_steps * per_step
    first_slot = (pl.program_id(0) * pl.num_programs(1) + pl.program_id(1)) * per_step
    levels = exchanges[0].all_levels if first_pass else exchanges[0].levels

    def all_copy(level):
        index = 0
        for lower in range(len(exchanges[0].bits)):
            index = index + exchanges[0].place(lower)[0] * (1 << lower)
        if level < 0:
            return all_s.at[pl.ds(index, 1)]
        size = 1 << level
        piece = all_s.at[pl.ds((index // size) * size, size)]
        return exchanges[0].copy(piece, piece, all_sends, all_recvs, level)

    def reduce_action(order):
        if order == 0:
            exchanges[0].barrier()
            own = all_copy(-1)
            own[...] = sums_ref[...][None]
        else:
            all_copy(order - 1).wait()
        if order < levels:
            all_copy(order).start()
        else:
            all_ref[...] = all_s[...]
        for exchange, state, shard in zip(exchanges, states, shards):
            if order > 0:
                exchange.reduce_finish(order - 1, *state)
            if order < levels:
                exchange.reduce_start(order, *state)
            else:
                shard[...] = exchange.own_shard(state[1], 1)[...][0]

    def gather_action(order):
        if order == 0:
            exchanges[0].barrier()
        for exchange, state, shard in zip(exchanges, states, shards):
            if order == 0:
                exchange.own_shard(state[0], 0)[...] = shard[...][None]
            else:
                exchange.gather_finish(levels - order, *state)
            if order < levels:
                exchange.gather_start(levels - 1 - order, *state)
        if order == levels:
            copies = [
                pltpu.make_async_copy(state[0], full, refs[index])
                for index, (state, full) in enumerate(zip(states, fulls))
            ]
            for copy in copies:
                copy.start()
            for copy in copies:
                copy.wait()

    action = reduce_action if first_pass else gather_action
    weights = [5.0, 10.0, 9.0, 6.0] + [4.0] * levels
    weights = weights[:levels] if first_pass else weights[:levels][::-1]
    marks, total = [0], 0.0
    for weight in weights:
        total += weight
        marks.append(total)
    last = static_slots - (2 if first_pass else 1)
    marks = [min(int(mark * last / total + 0.5), last) for mark in marks]

    dq_s[...] = jnp.zeros_like(dq_s) if first_pass else dq_in[0, 0].T

    def block(index, carry):
        for order, mark in enumerate(marks[:-1]):
            pl.when(first_slot + index == mark)(functools.partial(action, order))
        at = pl.ds(pl.multiple_of(index * rows, rows), rows)
        keys = k_ref[0, 0, at, :]
        values = v_ref[0, 0, at, :]
        lane = lane_index(keys.shape)
        low = lane < HD
        ones = jnp.where(lane % HD < 3, 1.0, 0.0).astype(BF16)
        zero = jnp.zeros_like(keys)
        grads = []
        for head in range(2):
            own = low if head == 0 else jnp.logical_not(low)
            query = qe_ref[0, 0, head]
            grad = ge_ref[0, 0, head]
            probs = jnp.exp(dot(jnp.where(own, keys, ones), query, NT))
            grad_probs = dot(jnp.where(own, values, ones), grad, NT)
            grad_scores = (probs * grad_probs).astype(BF16)
            grads.append((dot(grad_scores, query), dot(probs.astype(BF16), grad)))
            dq_s[...] += dot(jnp.where(own, keys, zero), grad_scores, TN)
        dk_ref[0, 0, at, :] = jnp.where(low, grads[0][0], grads[1][0]).astype(BF16)
        dv_ref[0, 0, at, :] = jnp.where(low, grads[0][1], grads[1][1]).astype(BF16)
        return carry

    lax.fori_loop(0, per_step, block, 0)
    if first_pass:
        dq_ref[0, 0] = dq_s[...].T
    else:
        dq_ref[0, 0] = (dq_s[...].T * HD**-0.5).astype(BF16)
    pl.when(first_slot + per_step == static_slots)(functools.partial(action, levels))


def joining(at, read, write, wait, own_ref, got_ref, out_ref, own_s, got_s, sems):
    mine = first_step(2)
    reads = [
        pltpu.make_async_copy(own_ref, own_s, sems.at[0]),
        pltpu.make_async_copy(got_ref, got_s, sems.at[1]),
    ]
    writes = [
        pltpu.make_async_copy(own_s, out_ref.at[pl.ds(mine, 2)], sems.at[2]),
        pltpu.make_async_copy(got_s, out_ref.at[pl.ds(2 - mine, 2)], sems.at[3]),
    ]

    @pl.when(at == read)
    def _():
        for copy in reads:
            copy.start()

    @pl.when(at == write)
    def _():
        for copy in reads:
            copy.wait()
        for copy in writes:
            copy.start()

    @pl.when(at == wait)
    def _():
        for copy in writes:
            copy.wait()


def project_back_far_kernel(
    dk_ref, dv_ref, normed_ref, w_ref, own_ref, got_ref, dx_ref, gw_ref, out_ref, own_s, got_s, sems
):
    width = w_ref.shape[0]
    at = pl.program_id(0) * pl.num_programs(1) + pl.program_id(1)
    joining(at, 0, 1, 3, own_ref, got_ref, out_ref, own_s, got_s, sems)
    joined = join_heads(dk_ref, dv_ref)
    dx_ref[0, 0] = dot(joined, w_ref[:, width:], NT).astype(BF16)

    @pl.when((pl.program_id(0) == 0) & (pl.program_id(1) == 0))
    def _():
        gw_ref[...] = jnp.zeros_like(gw_ref)

    gw_ref[...] += dot(normed_ref[0, 0], joined, TN)


def weight_back_kernel(early, *refs):
    dq_ref, dk_ref, dv_ref, normed_ref, far_ref, one_ref, two_ref = refs[:7]
    gw_ref, gfc1_ref, gfc2_ref, gout_ref = refs[7:11]
    gw_s, one_s, two_s, gfc1_s, gfc2_s, gout_s, sems = refs[11:]
    at = pl.program_id(0) * pl.num_programs(1) + pl.program_id(1)
    size = gout_s.shape[0]
    blocks = gfc1_s.shape[1] // size
    reads = [
        pltpu.make_async_copy(one_ref, one_s, sems.at[0]),
        pltpu.make_async_copy(two_ref, two_s, sems.at[1]),
    ]
    writes = [
        pltpu.make_async_copy(gfc1_s, gfc1_ref, sems.at[2]),
        pltpu.make_async_copy(gfc2_s, gfc2_ref, sems.at[3]),
        pltpu.make_async_copy(gout_s, gout_ref, sems.at[4]),
    ]

    @pl.when(at == 0)
    def _():
        for copy in reads:
            copy.start()

    @pl.when(at == 1)
    def _():
        reads[0].wait()
        unstack(
            grouped(early[0]), one_s, [(gfc1_s, 0, block * size) for block in range(blocks)], size
        )
        writes[0].start()

    @pl.when(at == 2)
    def _():
        reads[1].wait()
        rest = [(gfc2_s, block * size, 0) for block in range(blocks)] + [(gout_s, 0, 0)]
        unstack(grouped(early[1]), two_s, rest, size)
        writes[1].start()
        writes[2].start()

    @pl.when(at == pl.num_programs(0) * pl.num_programs(1) - 1)
    def _():
        for copy in writes:
            copy.wait()

    step, which = pl.program_id(0), pl.program_id(1)
    width = normed_ref.shape[3]

    @pl.when((step == 0) & (which == 0))
    def _():
        gw_s[:, :width] = jnp.zeros_like(gw_s[:, :width])
        gw_s[:, width:] = far_ref[...]

    gw_s[...] += dot(normed_ref[0, 0], join_heads(dq_ref, dk_ref, dv_ref), TN)

    @pl.when((step == pl.num_programs(0) - 1) & (which == pl.num_programs(1) - 1))
    def _():
        for block in range(gw_ref.shape[0]):
            gw_ref[block] = gw_s[:, block * LANES : (block + 1) * LANES].astype(BF16)


def join_heads(*grads):
    return jnp.concatenate([ref[0, pair] for ref in grads for pair in range(ref.shape[1])], axis=-1)


class Direct:
    def __init__(self, mesh_shape, row_tiles):
        self.chips = mesh_shape["seq"] // 2
        self.peers = mesh_shape["dp"] * self.chips
        self.half = row_tiles * 8
        self.piece = -(-row_tiles // (2 * self.peers)) * 16
        self.padded = self.piece * self.peers

    def me(self):
        return lax.axis_index("dp") * self.chips + lax.axis_index("seq") // 2

    def core(self):
        return lax.axis_index("seq") % 2

    def sibling(self):
        return {"seq": lax.axis_index("seq") + 1 - 2 * self.core()}

    def peer(self, shift):
        other = (self.me() + shift) % self.peers
        device = {"dp": other // self.chips, "seq": (other % self.chips) * 2 + self.core()}
        return other, device

    def rows(self, index):
        return pl.ds(pl.multiple_of(index * self.piece, 16), self.piece)

    def barrier(self):
        semaphore = pltpu.get_barrier_semaphore()

        def signal(device):
            pl.semaphore_signal(semaphore, 1, device_id=device, device_id_type=pl.DeviceIdType.MESH)

        signal(self.sibling())

        def greet(shift, carry):
            signal(self.peer(shift)[1])
            return carry

        lax.fori_loop(1, self.peers, greet, 0)
        pl.semaphore_wait(semaphore, self.peers)

    def copy(self, source, target, send, recv, device):
        return pltpu.make_async_remote_copy(
            src_ref=source,
            dst_ref=target,
            send_sem=send,
            recv_sem=recv,
            device_id=device,
            device_id_type=pl.DeviceIdType.MESH,
        )

    def each_peer(self, do):
        def one(shift, carry):
            do(shift)
            return carry

        lax.fori_loop(1, self.peers, one, 0)


def tail_kernel(direct, remote, *refs):
    give_ref, own_x, sib_x, mod_ref, lead_ref, gm_ref, dq_ref, dk_ref, dv_ref, w_ref = refs[:10]
    others = refs[10 : 10 + remote]
    grad_ref, got_ref, full_ref, all_ref = refs[10 + remote : 14 + remote]
    sums_s, other_s, got_s, sum_s, core_s, pieces_s, full_s, all_s = refs[14 + remote : 22 + remote]
    core_sems, piece_sems, back_sems, all_sems, grad_sems, local_sem = refs[22 + remote :]
    step, half = pl.program_id(0), pl.program_id(1)
    width = own_x.shape[2]
    core, me = direct.core(), direct.me()

    core_copy = direct.copy(
        give_ref.at[1 - core], core_s, core_sems.at[0], core_sems.at[1], direct.sibling()
    )

    def piece_copy(shift):
        other, device = direct.peer(shift)
        return direct.copy(
            sum_s.at[direct.rows(other)],
            pieces_s.at[shift],
            piece_sems.at[0, shift],
            piece_sems.at[1, shift],
            device,
        )

    def full_copy(shift, arriving):
        _, device = direct.peer(shift)
        owner = (me + direct.peers - shift) % direct.peers if arriving else me
        place = full_s.at[core, direct.rows(owner)]
        return direct.copy(place, place, back_sems.at[0, shift], back_sems.at[1, shift], device)

    def sums_copy(shift, arriving):
        _, device = direct.peer(shift)
        owner = (me + direct.peers - shift) % direct.peers if arriving else me
        place = all_s.at[core, owner]
        return direct.copy(place, place, all_sems.at[0, shift], all_sems.at[1, shift], device)

    def side_copy(values, which, side):
        place = values.at[side]
        return direct.copy(
            place, place, core_sems.at[which], core_sems.at[which + 1], direct.sibling()
        )

    def grad_copy(index):
        return direct.copy(
            other_s.at[index],
            got_s.at[index],
            grad_sems.at[0, index],
            grad_sems.at[1, index],
            direct.sibling(),
        )

    @pl.when((step == 0) & (half == 0))
    def _():
        direct.barrier()
        core_copy.start()
        sums_s[...] = jnp.zeros_like(sums_s)

    @pl.when((step == 0) & (half == 1))
    def _():
        core_copy.wait()
        real = core_s.shape[0]
        sum_s[:real] = (give_ref[core].astype(F32) + core_s[...].astype(F32)).astype(BF16)
        if direct.padded > real:
            sum_s[real:] = jnp.zeros_like(sum_s[real:])
        direct.each_peer(lambda shift: piece_copy(shift).start())

    x = jnp.where(half == 0, own_x[0], sib_x[0]).astype(F32)
    scale = mod_ref[pl.ds(step, 1), width : 2 * width]
    xhat, inverse = normalize(x)
    gy = dot(join_heads(dq_ref, dk_ref, dv_ref), w_ref[...], NT)
    for other in others:
        gy = gy + other[0, 0].astype(F32)
    grad = (gm_ref[0, 0] + norm_back(gy * (1.0 + scale), xhat, inverse)).astype(BF16)

    @pl.when(half == 0)
    def _():
        grad_ref[0] = grad

    @pl.when(half == 1)
    def _():
        other_s[step] = grad
        grad_copy(step).start()

    for kind, value in enumerate((gy, gy * xhat)):
        total = jnp.sum(value, axis=0, keepdims=True)
        for index in range(width // LANES):
            place = pl.ds((kind * 2 + step) * (width // LANES) + index, 1)
            sums_s[place, :] += total[:, index * LANES : (index + 1) * LANES]

    @pl.when((step == 1) & (half == 1))
    def _():
        for index in range(2):
            chosen = lane_index((1, LANES)) == lead_ref[0, first_step(2) + index]
            sums_s[12 + index : 13 + index, :] = jnp.where(chosen, 1.0, 0.0)
        all_s[core, me] = sums_s[...].astype(BF16)
        direct.each_peer(lambda shift: sums_copy(shift, False).start())
        direct.each_peer(lambda shift: piece_copy(shift).wait())

        def add(shift, total):
            return total + pieces_s[shift].astype(F32)

        total = lax.fori_loop(1, direct.peers, add, sum_s[direct.rows(me)].astype(F32))
        full_s[core, direct.rows(me)] = total.astype(BF16)
        direct.each_peer(lambda shift: full_copy(shift, False).start())

        def arrived(shift):
            full_copy(shift, False).wait_send()
            full_copy(shift, True).wait_recv()
            sums_copy(shift, False).wait_send()
            sums_copy(shift, True).wait_recv()

        direct.each_peer(arrived)
        side_copy(full_s, 2, core).start()
        side_copy(all_s, 4, core).start()
        for index in range(2):
            grad_copy(index).wait()
        side_copy(full_s, 2, core).wait_send()
        side_copy(full_s, 2, 1 - core).wait_recv()
        side_copy(all_s, 4, core).wait_send()
        side_copy(all_s, 4, 1 - core).wait_recv()
        outs = [(got_s, got_ref), (full_s, full_ref), (all_s, all_ref)]
        copies = [
            pltpu.make_async_copy(source, target, local_sem.at[index])
            for index, (source, target) in enumerate(outs)
        ]
        for copy in copies:
            copy.start()
        for copy in copies:
            copy.wait()


def unstack(at, full_ref, targets, rows):
    row, end = 0, rows * len(targets)
    while row < end:
        group, inside, left = at(row)
        block, place = divmod(row, rows)
        count = min(left, rows - place)
        target, first_row, first_column = targets[block]
        columns = slice(first_column, first_column + full_ref.shape[2])
        value = full_ref[group, inside : inside + count, :].astype(F32)
        target[first_row + place : first_row + place + count, columns] = value
        row += count


def grouped(exchange):
    def at(row):
        group, inside = divmod(row, exchange.real)
        return group, inside, exchange.real - inside

    return at


def spread_leads(grads, step_of, table_rows):
    count = grads.shape[0]
    part = min(count, 512)
    row = lax.broadcasted_iota(jnp.int32, (part, part), 0)
    column = lane_index((part, part))
    chosen = (row // 16 == column // 16) & (row % 16 == 12 + step_of(column % 16))
    spread = jnp.where(chosen, 1.0, 0.0).astype(BF16)
    leads = [
        dot(grads[start : start + part, :LANES], spread, TN)[:table_rows]
        for start in range(0, count, part)
    ]
    return jnp.concatenate(leads, axis=-1)


def final_kernel(direct, *refs):
    early_sums, late_sums, emb_ref, ada_ref, late_ref, own_ref, got_ref = refs[:7]
    grad_out, gemb_ref, gada_out, gbada_ref, gqkv_out = refs[7:12]
    gada_s, gqkv_s, late_s, own_s, got_s, sems = refs[12:]
    size = emb_ref.shape[1]
    mine = first_step(2)
    pairs = [(late_ref, late_s), (own_ref, own_s), (got_ref, got_s)]
    reads = [
        pltpu.make_async_copy(source, target, sems.at[index])
        for index, (source, target) in enumerate(pairs)
    ]
    for read in reads:
        read.start()
    copies = []

    def start(source, target):
        copy = pltpu.make_async_copy(source, target, sems.at[3 + len(copies)])
        copy.start()
        copies.append(copy)

    def halved(row):
        group, inside = divmod(row, direct.half)
        return group, inside, direct.half - inside

    columns = gqkv_s.shape[1] // LANES
    reads[0].wait()
    unstack(halved, late_s, [(gqkv_s, 0, block * LANES) for block in range(columns)], size)
    start(gqkv_s, gqkv_out)
    reads[1].wait()
    start(own_s, grad_out.at[pl.ds(mine, 2)])
    reads[2].wait()
    start(got_s, grad_out.at[pl.ds(2 - mine, 2)])

    table_rows = emb_ref.shape[0]
    table = emb_ref[...].astype(F32)
    gate = jax.nn.sigmoid(table)
    slope = gate * (1.0 + table * (1.0 - gate))
    table_act = (table * gate).astype(BF16)
    total = jnp.zeros((table_rows, size), F32)

    def one_piece(grads, leads, place, first):
        chosen = jnp.where(place, leads, 0.0).astype(BF16)
        acts = dot(table_act, chosen, TN).astype(BF16)
        where = slice(first, first + grads.shape[1])
        gada_s[:, where] = dot(acts, grads)
        by_lead = dot(chosen, grads)
        gbada_ref[where] = jnp.sum(by_lead, axis=0)
        high = by_lead.astype(BF16)
        low = (by_lead - high.astype(F32)).astype(BF16)
        return dot(high, ada_ref[:, where], NT) + dot(low, ada_ref[:, where], NT)

    grads = early_sums[...]
    leads = spread_leads(grads, lambda row: row % 2, table_rows)
    row = lane_index((1, grads.shape[0])) % 16
    for index in range(4):
        total += one_piece(grads, leads, row // 2 == index, (2 + index) * size)
    grads = late_sums[...]
    parts = size // LANES
    leads = spread_leads(grads, lambda row: (row // parts) % 2, table_rows)
    row = lane_index((1, grads.shape[0])) % 16
    for index in range(2):
        for part in range(parts):
            place = (row // (2 * parts) == index) & (row % parts == part)
            total += one_piece(grads, leads, place, index * size + part * LANES)
    gemb_ref[...] = total * slope
    start(gada_s, gada_out)
    for copy in copies:
        copy.wait()


def local(
    mesh_shape, inputs, cotangent, counts, lead_steps, emb_table, w_ada, b_ada, w_qkv, w_out, w_fc1, w_fc2
):
    slots, items, patches, width = inputs.shape
    chips = mesh_shape["seq"] // 2
    blocks = w_fc1.shape[1] // w_fc1.shape[0]
    steps = slots * items // 2
    hidden_width = w_fc1.shape[1]
    pairs = width // LANES
    rows = 2 * patches
    remote = 2 * (chips - 1)
    far_rows = remote * patches
    spot = lax.axis_index("seq")
    core = lax.rem(spot, 2)
    devices = 2 * chips

    def send(values, shift, cross):
        pairs_list = []
        for source in range(devices):
            chip, side = source // 2, source % 2
            pairs_list.append((source, ((chip + shift) % chips) * 2 + (1 - side if cross else side)))
        return lax.ppermute(values, "seq", pairs_list)

    x_steps = inputs.reshape(2, steps, patches, width)
    ct_steps = cotangent.reshape(2, steps, patches, width)
    own_x = lax.dynamic_index_in_dim(x_steps, core, 0, keepdims=False)
    other_x = lax.dynamic_index_in_dim(x_steps, 1 - core, 0, keepdims=False)
    own_ct = lax.dynamic_index_in_dim(ct_steps, core, 0, keepdims=False)
    other_ct = lax.dynamic_index_in_dim(ct_steps, 1 - core, 0, keepdims=False)
    sib_x = send(other_x, 0, True)
    far_x = []
    for step in range(steps):
        some = slice(step, step + 1)
        for shift in range(1, chips):
            far_x.append(send(own_x[some], shift, False))
            far_x.append(send(other_x[some], shift, True))
    sib_ct = send(other_ct, 0, True)

    step_block = pl.BlockSpec((1, patches, width), lambda j, i: (j, 0, 0))
    patch_block = pl.BlockSpec((1, 1, patches, width), lambda j, i: (j, i, 0, 0))

    def head_rows(count):
        return pl.BlockSpec((1, 1, count, LANES), lambda j, p: (j, p, 0, 0))

    def of_step(*shape):
        return pl.BlockSpec((1,) + shape, lambda j, p: (j,) + (0,) * len(shape))

    both_heads = pl.BlockSpec((1, 1, 2, rows, LANES), lambda j, p: (j, p, 0, 0, 0))
    piece = min(256, rows)
    near_work = 4 * steps * pairs * 2 * rows * LANES * rows
    near_heads = jax.ShapeDtypeStruct((steps, pairs, rows, LANES), BF16)
    mod, n1, q, k, v, acc = call(
        functools.partial(near_kernel, piece),
        "near",
        (steps, pairs),
        [scalars(), whole(emb_table.shape), whole(w_ada.shape), whole((1, 6 * width))]
        + [step_block] * 2
        + [whole(w_qkv.shape)],
        [whole((16, 6 * width)), of_step(rows, width)]
        + [of_step(pairs, rows, LANES)] * 3
        + [both_heads],
        [
            jax.ShapeDtypeStruct((16, 6 * width), F32),
            jax.ShapeDtypeStruct((steps, rows, width), BF16),
            near_heads,
            near_heads,
            near_heads,
            jax.ShapeDtypeStruct((steps, pairs, 2, rows, LANES), F32),
        ],
        [pltpu.VMEM((2, rows, LANES), BF16)],
        flops=near_work + 6 * steps * rows * width * width,
        exps=steps * pairs * 2 * rows * rows,
    )(lead_steps, emb_table, w_ada, b_ada.reshape(1, -1), own_x, sib_x, w_qkv)

    def far(step, before):
        some_x = far_x[step * remote : (step + 1) * remote]

        def at_step(*shape):
            return pl.BlockSpec((1,) + shape, lambda p: (step,) + (0,) * len(shape))

        def at_pair(*shape):
            return pl.BlockSpec((1, 1) + shape, lambda p: (step, p) + (0,) * len(shape))

        operands = [*some_x, mod, w_qkv, q, k, v, acc]
        return call(
            functools.partial(far_kernel, piece, step, remote),
            "far",
            (pairs,),
            [whole((1, patches, width))] * remote
            + [whole(mod.shape), whole(w_qkv.shape)]
            + [at_pair(rows, LANES)] * 3
            + [at_pair(2, rows, LANES)]
            + [pl.BlockSpec(memory_space=pl.ANY)] * len(before),
            [at_step(far_rows, width)]
            + [at_step(pairs, far_rows, LANES)] * 2
            + [at_pair(rows, LANES), at_pair(2, rows, LANES)],
            [
                jax.ShapeDtypeStruct((steps, far_rows, width), BF16),
                jax.ShapeDtypeStruct((steps, pairs, far_rows, LANES), BF16),
                jax.ShapeDtypeStruct((steps, pairs, far_rows, LANES), BF16),
                jax.ShapeDtypeStruct((steps, pairs, rows, LANES), F32),
                jax.ShapeDtypeStruct((steps, pairs, 2, rows, LANES), BF16),
            ],
            [pltpu.VMEM((2, far_rows, LANES), BF16), pltpu.VMEM((rows, LANES), F32)],
            flops=near_work // 2,
            exps=pairs * 2 * rows * far_rows,
            aliases={len(operands) + index: index for index in range(len(before))},
        )(*operands, *before)

    far_results = []
    for step in range(steps):
        far_results = far(step, far_results)
    n1r, kr, vr, o, qe = far_results

    block_rows = min(256, patches)
    outs = call(
        functools.partial(patch_kernel, block_rows, hidden_width),
        "patchwise",
        (steps, 2),
        [scalars()] * 2
        + [step_block] * 4
        + [
            whole(mod.shape),
            pl.BlockSpec((1, pairs, patches, LANES), lambda j, i: (j, 0, i, 0)),
            whole(w_out.shape),
            whole(w_fc1.shape),
            whole(w_fc2.shape),
        ],
        [
            step_block,
            step_block,
            patch_block,
            pl.BlockSpec((1, pairs, 2, patches, LANES), lambda j, i: (j, 0, 0, i, 0)),
            whole((16, width)),
            whole((blocks, width, width)),
            whole((blocks + 1, width, width)),
        ],
        [
            jax.ShapeDtypeStruct((steps, patches, width), BF16),
            jax.ShapeDtypeStruct((steps, patches, width), BF16),
            jax.ShapeDtypeStruct((steps, 2, patches, width), F32),
            jax.ShapeDtypeStruct((steps, pairs, 2, rows, LANES), BF16),
            jax.ShapeDtypeStruct((16, width), BF16),
            jax.ShapeDtypeStruct((blocks, width, width), BF16),
            jax.ShapeDtypeStruct((blocks + 1, width, width), BF16),
        ],
        [pltpu.VMEM((patches, hidden_width), BF16)] * 2
        + [pltpu.VMEM((patches, width), BF16)] * 4
        + [
            pltpu.VMEM((width, width), F32),
            pltpu.VMEM((width, hidden_width), F32),
            pltpu.VMEM((width, hidden_width), F32),
            pltpu.VMEM((16, width), F32),
        ],
        flops=6 * steps * rows * width * (2 * hidden_width + width),
        moved=steps * rows * width * 20,
        exps=2 * steps * rows * hidden_width,
    )(counts, lead_steps, own_x, sib_x, own_ct, sib_ct, mod, o, w_out, w_fc1, w_fc2)
    final_own, final_sib, gm, ge, sums, stack_one, stack_two = outs
    final_got = send(final_sib, 0, True)
    early = [Exchange(mesh_shape, blocks * width // 16, 0), Exchange(mesh_shape, (blocks + 1) * width // 16, 1)]
    gives = [g.reshape(e.groups, e.real, width) for e, g in zip(early, (stack_one, stack_two))]

    def attend_back(keys, values, extra, first, name):
        count = keys.shape[2]
        in_specs = [both_heads] * 2 + [head_rows(count)] * 2
        out_specs = [head_rows(rows), head_rows(count), head_rows(count)]
        out_shape = [
            jax.ShapeDtypeStruct((steps, pairs, rows, LANES), F32 if first else BF16),
            jax.ShapeDtypeStruct((steps, pairs, count, LANES), BF16),
            jax.ShapeDtypeStruct((steps, pairs, count, LANES), BF16),
        ]
        scratch = [pltpu.VMEM((LANES, rows), F32)]
        if not first:
            in_specs += [head_rows(rows)]
        for exchange in early:
            shape = (exchange.groups, exchange.padded, width)
            shard = (exchange.shard, width)
            sems = [pltpu.SemaphoreType.DMA((exchange.all_levels,))] * 2
            if first:
                in_specs += [whole((exchange.groups, exchange.real, width))]
                out_specs += [whole(shard)]
                out_shape += [jax.ShapeDtypeStruct(shard, BF16)]
                half = (exchange.groups // 2, exchange.padded, width)
                scratch += [pltpu.VMEM(half, BF16)] + sems + exchange.receive_scratch(width)
            else:
                in_specs += [whole(shard)]
                out_specs += [pl.BlockSpec(memory_space=pl.ANY)]
                out_shape += [jax.ShapeDtypeStruct(shape, BF16)]
                scratch += [pltpu.VMEM(shape, BF16)] + sems
        if first:
            every = (mesh_shape["dp"] * mesh_shape["seq"], 16, width)
            in_specs += [whole(sums.shape)]
            out_specs += [whole(every)]
            out_shape += [jax.ShapeDtypeStruct(every, BF16)]
            sems = [pltpu.SemaphoreType.DMA((early[0].all_levels,))] * 2
            scratch += [pltpu.VMEM(every, BF16)] + sems
        else:
            scratch += [pltpu.SemaphoreType.DMA] * len(early)
        return call(
            functools.partial(attend_back_kernel, min(512, count), first, early, steps * pairs),
            name,
            (steps, pairs),
            in_specs,
            out_specs,
            out_shape,
            scratch,
            flops=10 * steps * pairs * 2 * rows * count * LANES,
            exps=steps * pairs * 2 * rows * count,
            collective=1 if first else 2,
        )(qe, ge, keys, values, *extra)

    grad_block = pl.BlockSpec((1, pairs, patches, LANES), lambda j, i: (j, 0, i, 0))
    hbm = pl.BlockSpec(memory_space=pl.ANY)

    dq_part, dkr, dvr, shard_one, shard_two, early_all = attend_back(
        kr, vr, [*gives, sums], True, "attend_back_far"
    )
    dx_far, gw_part, outputs = call(
        project_back_far_kernel,
        "project_back_far",
        (steps, remote),
        [grad_block] * 2 + [patch_block, whole(w_qkv.shape), hbm, hbm],
        [patch_block, whole((width, 2 * width)), hbm],
        [
            jax.ShapeDtypeStruct((steps, remote, patches, width), BF16),
            jax.ShapeDtypeStruct((width, 2 * width), F32),
            jax.ShapeDtypeStruct((2 * steps, patches, width), BF16),
        ],
        [pltpu.VMEM((steps, patches, width), BF16)] * 2 + [pltpu.SemaphoreType.DMA((4,))],
        flops=4 * steps * far_rows * width * 2 * width,
        moved=steps * far_rows * width * 8,
    )(dkr, dvr, n1r.reshape(steps, remote, patches, width), w_qkv, final_own, final_got)
    dx_got = [send(dx_far[:, 2 * r - 2 : 2 * r], -r, False) for r in range(1, chips)]
    dq, dk, dv, *early_sums = attend_back(
        k, v, [dq_part, shard_one, shard_two], False, "attend_back_near"
    )
    columns = w_qkv.shape[1] // LANES
    early_weights = (w_fc1, w_fc2, w_out)
    give_late, g_fc1, g_fc2, g_out = call(
        functools.partial(weight_back_kernel, early),
        "weight_back",
        (steps, 2),
        [grad_block] * 3 + [patch_block, whole(gw_part.shape), hbm, hbm],
        [whole((columns, width, LANES))] + [hbm] * 3,
        [jax.ShapeDtypeStruct((columns, width, LANES), BF16)]
        + [jax.ShapeDtypeStruct(w.shape, F32) for w in early_weights],
        [pltpu.VMEM((width, columns * LANES), F32)]
        + [pltpu.VMEM(value.shape, BF16) for value in early_sums]
        + [pltpu.VMEM(w.shape, F32) for w in early_weights]
        + [pltpu.SemaphoreType.DMA((5,))],
        flops=2 * steps * rows * width * 3 * width,
        moved=steps * rows * width * 8,
    )(dq, dk, dv, n1.reshape(steps, 2, patches, width), gw_part, *early_sums)

    direct = Direct(mesh_shape, columns * width // 16)
    full_shape = (2, direct.padded, LANES)
    late_all_shape = (2, direct.peers, 16, LANES)
    grad_own, grad_got, late_sum, late_all = call(
        functools.partial(tail_kernel, direct, len(dx_got)),
        "tail",
        (steps, 2),
        [whole((2, direct.half, LANES)), step_block, step_block, whole(mod.shape), scalars()]
        + [patch_block]
        + [grad_block] * 3
        + [whole(w_qkv.shape)]
        + [patch_block] * len(dx_got),
        [step_block, hbm, hbm, hbm],
        [
            jax.ShapeDtypeStruct((steps, patches, width), BF16),
            jax.ShapeDtypeStruct((steps, patches, width), BF16),
            jax.ShapeDtypeStruct(full_shape, BF16),
            jax.ShapeDtypeStruct(late_all_shape, BF16),
        ],
        [
            pltpu.VMEM((16, LANES), F32),
            pltpu.VMEM((steps, patches, width), BF16),
            pltpu.VMEM((steps, patches, width), BF16),
            pltpu.VMEM((direct.padded, LANES), BF16),
            pltpu.VMEM((direct.half, LANES), BF16),
            pltpu.VMEM((direct.peers, direct.piece, LANES), BF16),
            pltpu.VMEM(full_shape, BF16),
            pltpu.VMEM(late_all_shape, BF16),
            pltpu.SemaphoreType.DMA((6,)),
            pltpu.SemaphoreType.DMA((2, direct.peers)),
            pltpu.SemaphoreType.DMA((2, direct.peers)),
            pltpu.SemaphoreType.DMA((2, direct.peers)),
            pltpu.SemaphoreType.DMA((2, steps)),
            pltpu.SemaphoreType.DMA((3,)),
        ],
        flops=2 * steps * rows * width * 3 * width,
        collective=3,
    )(
        give_late.reshape(2, direct.half, LANES),
        own_x,
        sib_x,
        mod,
        lead_steps,
        gm,
        dq,
        dk,
        dv,
        w_qkv,
        *dx_got,
    )

    early_all = early_all.reshape(-1, width)
    late_all = late_all.reshape(-1, LANES)
    small = [early_all, late_all, emb_table, w_ada]
    large = [late_sum, grad_own, grad_got]
    out_shapes = [(slots * items, patches, width), emb_table.shape, w_ada.shape, b_ada.shape, w_qkv.shape]
    grad_inputs, g_emb, g_ada, g_bada, g_qkv = call(
        functools.partial(final_kernel, direct),
        "final",
        (),
        [whole(value.shape) for value in small] + [hbm] * len(large),
        [hbm, whole(emb_table.shape), hbm, whole(b_ada.shape), hbm],
        [
            jax.ShapeDtypeStruct(shape, F32 if index else BF16)
            for index, shape in enumerate(out_shapes)
        ],
        [pltpu.VMEM(w.shape, F32) for w in (w_ada, w_qkv)]
        + [pltpu.VMEM(value.shape, BF16) for value in large]
        + [pltpu.SemaphoreType.DMA((7,))],
        flops=2 * early_all.shape[0] * width * 6 * width,
        moved=6 * w_ada.size,
    )(*small, *large)
    return (
        outputs.reshape(inputs.shape),
        grad_inputs.reshape(inputs.shape),
        g_emb,
        g_ada,
        g_bada,
        g_qkv,
        g_out,
        g_fc1,
        g_fc2,
    )


def solution(mesh):
    tokens = P(None, "dp", "seq", None)
    return jax.shard_map(
        functools.partial(local, dict(mesh.shape)),
        mesh=mesh,
        in_specs=(tokens, tokens, P("dp"), P("dp", None)) + (P(),) * 7,
        out_specs=(tokens, tokens) + (P(),) * 7,
        check_vma=False,
    )
```

profile of v0, /device:TPU:27, one launch (start us, length us, event | category | flops | bytes accessed | tf_op | source)
XLA Modules:
  0.0 218.5 jit_solution(7858186605933813119)
XLA Ops:
  0.7 0.0 copy-start.15
  0.7 2.5 %dynamic-slice_bitcast_fusion.2 = (bf16[2,512,384]{2,1,0:T(8,128)(2,1)}, bf16[2,512,384]{2,1,0:T(8,128)(2,1)S(1)}) fusion(bf16[2,2,512,384]{3,2,1,0:T(8,128)(2,1)} %bitcast.38, s32[]{:T(128)S(6)} %select_n.10, s32[]{:T(128)S(6)} %select_n.9), kind=kLoop, calls=%fused_computation.2 | loop fusion | bytes 3145736 | tf_op jit(solution)/shard_map/jit(dynamic_index_in_dim)/squeeze | solution.py:1064
  3.2 0.7 collective-permute-start.2
  3.9 0.0 copy-done.15
  3.9 0.0 copy-start.17
  3.9 0.0 copy-start.16
  3.9 0.2 dynamic-slice_bitcast_fusion.4
  4.0 1.3 collective-permute-start.3
  5.3 0.4 collective-permute-start.4
  5.8 1.2 collective-permute-start
  7.0 0.6 collective-permute-start.1
  7.6 0.0 copy-done.17
  8.3 0.0 copy-done.16
  8.3 0.0 copy-start
  8.3 0.0 copy-start.1
  8.3 0.0 copy-start.10
  8.3 0.0 copy-start.11
  8.3 0.2 dynamic-slice_bitcast_fusion
  8.5 0.0 collective-permute-done.2.refs_5_.sib_x.refs_2_
  8.5 0.0 copy-start.7
  8.5 0.1 collective-permute-start.5
  8.6 0.9 copy-done
  9.5 0.8 copy-done.1
  10.3 0.0 copy-done.10
  10.3 0.0 copy-done.11
  10.3 19.1 %near.1 = (f32[16,2304]{1,0:T(8,128)S(1)}, bf16[2,1024,384]{2,1,0:T(8,128)(2,1)S(1)}, bf16[2,3,1024,128]{3,2,1,0:T(8,128)(2,1)S(1)}, bf16[2,3,1024,128]{3,2,1,0:...) custom-call(s32[1,4]{1,0:T(1,128)S(1)} %copy-done.11, ...), custom_call_target="tpu_custom_call" | custom-call | flops 8254390272 | tf_op jit(solution)/shard_map/near/pallas_call | solution.py:1089
  29.5 0.0 copy-done.7
  29.5 0.0 copy-start.3
  29.5 0.0 collective-permute-done.3.refs_0_
  29.5 0.0 collective-permute-done.4.refs_1_
  29.5 9.9 %far.2 = (bf16[2,1024,384]{2,1,0:T(8,128)(2,1)S(1)}, bf16[2,3,1024,128]{3,2,1,0:T(8,128)(2,1)S(1)}, bf16[2,3,1024,128]{3,2,1,0:T(8,128)(2,1)S(1)}, f32[2,3,1024,...) custom-call(bf16[1,512,384]{2,1,0:T(8,128)(2,1)S(1)} %collective-permute-done.3.refs_0_, ...), custom_call_target="tpu_custom_call" | custom-call | flops 3221225472 | tf_op jit(solution)/shard_map/far/pallas_call | solution.py:1122
  39.5 0.0 copy-done.3
  39.5 0.0 collective-permute-done.refs_0_
  39.5 0.7 collective-permute-done.1.refs_1_
  40.2 0.0 copy-start.8
  40.2 0.0 copy-start.12
  40.2 0.0 copy-start.14
  40.2 10.1 %far.3 = (bf16[2,1024,384]{2,1,0:T(8,128)(2,1)S(1)}, bf16[2,3,1024,128]{3,2,1,0:T(8,128)(2,1)S(1)}, bf16[2,3,1024,128]{3,2,1,0:T(8,128)(2,1)S(1)}, f32[2,3,1024,...) custom-call(bf16[1,512,384]{2,1,0:T(8,128)(2,1)S(1)} %collective-per, ...), custom_call_target="tpu_custom_call", output_to_operand_aliasing={{0}: (8, {}), {1}: (9, {}), {2}: (10, {}), {3}: (11, {}), {... | custom-call | flops 3221225472 | tf_op jit(solution)/shard_map/far/pallas_call | solution.py:1122
  50.4 0.0 copy-start.5
  50.4 1.1 copy-done.5
  51.5 0.0 collective-permute-done.5.sib_ct
  51.5 0.0 copy-done.8
  51.5 0.0 copy-done.12
  51.5 0.0 copy-done.13
  51.5 0.0 copy-done.14
  51.5 0.0 copy-start.6
  51.5 33.8 %patchwise.1 = (bf16[2,512,384]{2,1,0:T(8,128)(2,1)S(1)}, bf16[2,512,384]{2,1,0:T(8,128)(2,1)S(1)}, f32[2,2,512,384]{3,2,1,0:T(8,128)S(1)}, bf16[2,3,2,1024,128]...) custom-call(s32[1]{0:T(128)S(6)} %copy.32.counts_ref, ...), custom_call_target="tpu_custom_call" | custom-call | flops 16307453952 | bytes 15728640 | tf_op jit(solution)/shard_map/patchwise/pallas_call | solution.py:1153
  85.4 0.3 collective-permute-start.6
  85.7 0.0 copy-done.6
  85.7 39.5 %attend_back_far.1 = (f32[2,3,1024,128]{3,2,1,0:T(8,128)S(1)}, bf16[2,3,1024,128]{3,2,1,0:T(8,128)(2,1)S(1)}, bf16[2,3,1024,128]{3,2,1,0:T(8,128)(2,1)S(1)}, bf1...) custom-call(bf16[2,3,2,1024,128]{4,3,2,1,0:T(8,128)(2,1)S(1)} %get-tuple-element.69.refs_0_,, ...), custom_call_target="tpu_custom_call" | custom-call | flops 16106127360 | tf_op jit(solution)/shard_map/attend_back_far/pallas_call | solution.py:1237
  125.2 0.0 collective-permute-done.6.got_ref
  125.2 5.8 %project_back_far.1 = (bf16[2,2,512,384]{3,2,1,0:T(8,128)(2,1)S(1)}, f32[384,768]{1,0:T(8,128)S(1)}, bf16[4,512,384]{2,1,0:T(8,128)(2,1)}) custom-call(bf16[2,3,1024,128]{3,2,1,0:T(8,128)(2,1)S(1)} %get-tuple-element.77.dk_ref, bf16[2,3,1024,128]{3,2,1,0:T(8,128)(2,1)S(1)} %get-tuple-element.78.dv_ref, bf16[2,2,512,384]{3,2,1,0:T(8,128)(2,1)S(1)} %bitcast.32, ...), custom_call_target="tpu_custom_call" | custom-call | flops 2415919104 | bytes 6291456 | tf_op jit(solution)/shard_map/project_back_far/pallas_call | solution.py:1256
  131.0 1.3 collective-permute-start.7
  132.3 0.0 copy-start.4
  132.3 37.2 %attend_back_near.1 = (bf16[2,3,1024,128]{3,2,1,0:T(8,128)(2,1)S(1)}, bf16[2,3,1024,128]{3,2,1,0:T(8,128)(2,1)S(1)}, bf16[2,3,1024,128]{3,2,1,0:T(8,128)(2,1)S(1...) custom-call(bf16[2,3,2,1024,128]{4,3,2,1,0:T(8,128)(2,1)S(1)} %get-tuple-element.69.refs_0_, ...), custom_call_target="tpu_custom_call" | custom-call | flops 16106127360 | tf_op jit(solution)/shard_map/attend_back_near/pallas_call | solution.py:1237
  169.5 0.0 copy-done.4
  169.5 0.0 copy-start.9
  169.5 5.1 %weight_back.1 = (bf16[9,384,128]{2,1,0:T(8,128)(2,1)S(1)}, f32[384,1536]{1,0:T(8,128)}, f32[1536,384]{1,0:T(8,128)}, f32[384,384]{1,0:T(8,128)}) custom-call(bf16[2,3,1024,128]{3,2,1,0:T(8,128)(2,1)S(1)} %get-tuple-element.87.refs_0_.refs_6_, bf16[2,3,1024,128]{3,2,1,0:T(8,128)(2,1)S(1)} %get-tuple-element.88.refs_1_.refs_7_, ...), custom_call_target="tpu_custom_call" | custom-call | flops 1811939328 | bytes 6291456 | tf_op jit(solution)/shard_map/weight_back/pallas_call | solution.py:1277
  174.6 0.0 collective-permute-done.7.refs_10_
  174.6 0.0 copy-done.9
  174.6 0.0 copy-start.2
  174.6 35.5 %tail.1 = (bf16[2,512,384]{2,1,0:T(8,128)(2,1)S(1)}, bf16[2,512,384]{2,1,0:T(8,128)(2,1)S(1)}, bf16[2,1792,128]{2,1,0:T(8,128)(2,1)S(1)}, bf16[2,16,16,128]{3,2,1,0:T(8,128)(2,1)S(1)}) custom-call(bf16[2,1728,128]{2,1,0:T(8,128)(2,1)S(1)} %bitcast.33, bf16[2,512,384]{2,1,0:T(8,128)(2,1)S(1)} %get-tuple-element.125.refs_4_.own_x.refs_1_, ...), custom_call_target="tpu_custom_call" | custom-call | flops 1811939328 | tf_op jit(solution)/shard_map/tail/pallas_call | solution.py:1296
  210.1 0.0 copy-done.2
  210.2 8.2 %final.1 = (bf16[4,512,384]{2,1,0:T(8,128)(2,1)}, f32[16,384]{1,0:T(8,128)}, f32[384,2304]{1,0:T(8,128)}, f32[2304]{0:T(1024)}, f32[384,1152]{1,0:T(8,128)}) custom-call(bf16[512,384]{1,0:T(8,128)(2,1)S(1)} %bitcast.34, bf16[512,128]{1,0:T(8,128)(2,1)S(1)} %bitcast.35, bf16[16,384]{1,0:T(8,128)(2,1)S(1)} %copy-done.10, bf16[384,2304]{1,0:T(8,128)(2,1)S(1)} %copy-done.2, ...), custom_call_target="tpu_custom_call" | custom-call | flops 905969664 | bytes 5308416 | tf_op jit(solution)/shard_map/final/pallas_call | solution.py:1349
  (2 shorter events, 0.0 us)
Async XLA Ops:
  0.7 3.2 %copy-start.15 = (bf16[4,1,512,384]{3,2,1,0:T(8,128)(2,1)S(1)}, bf16[4,1,512,384]{3,2,1,0:T(8,128)(2,1)}, u32[]{:S(2)}) copy-start(bf16[4,1,512,384]{3,2,1,0:T(8,128)(2,1)} %param.11) | copy-start | bytes 4718596
  3.2 5.3 %collective-permute-start.2 = (bf16[2,512,384]{2,1,0:T(8,128)(2,1)}, bf16[2,512,384]{2,1,0:T(8,128)(2,1)S(1)}, u32[]{:S(2)}, u32[]{:S(2)}) collective-permute-start(bf16[2,512,384]{2,1,0:T(8,128)(2,1)} %get-tuple-element.124), channel_id=1, source_target_pairs={{0,1},{1,0},{2,3},{3,2},{4,5},{5,4},{6,7},{7,6},{8,9},{9,8},{10,11... | collective-permute-start | bytes 2359304 | tf_op jit(solution)/shard_map/ppermute | solution.py:1059
  3.9 3.7 %copy-start.17 = (bf16[2304]{0:T(1024)(128)(2,1)S(1)}, bf16[2304]{0:T(1024)(128)(2,1)}, u32[]{:S(2)}) copy-start(bf16[2304]{0:T(1024)(128)(2,1)} %param.17) | copy-start | bytes 13828
  3.9 4.4 %copy-start.16 = (bf16[4,1,512,384]{3,2,1,0:T(8,128)(2,1)S(1)}, bf16[4,1,512,384]{3,2,1,0:T(8,128)(2,1)}, u32[]{:S(2)}) copy-start(bf16[4,1,512,384]{3,2,1,0:T(8,128)(2,1)} %param.12) | copy-start | bytes 4718596
  4.0 25.5 %collective-permute-start.3 = (bf16[1,512,384]{2,1,0:T(8,128)(2,1)S(1)}, bf16[1,512,384]{2,1,0:T(8,128)(2,1)S(1)}, u32[]{:S(2)}, u32[]{:S(2)}) collective-permute-start(bf16[1,512,384]{2,1,0:T(8,128)(2,1)S(1)} %get-tuple-element.121), channel_id=1, source_target_pairs={{0,2},{1,3},{2,0},{3,1},{4,6},{5,7},{6,4},{7,5},{8,10},{9,11},{10,... | collective-permute-start | bytes 1179656 | tf_op jit(solution)/shard_map/ppermute | solution.py:1059
  5.3 24.2 %collective-permute-start.4 = (bf16[1,512,384]{2,1,0:T(8,128)(2,1)S(1)}, bf16[1,512,384]{2,1,0:T(8,128)(2,1)S(1)}, u32[]{:S(2)}, u32[]{:S(2)}) collective-permute-start(bf16[1,512,384]{2,1,0:T(8,128)(2,1)S(1)} %get-tuple-element.120), channel_id=1, source_target_pairs={{0,3},{1,2},{2,1},{3,0},{4,7},{5,6},{6,5},{7,4},{8,11},{9,10},{10,... | collective-permute-start | bytes 1179656 | tf_op jit(solution)/shard_map/ppermute | solution.py:1059
  5.8 33.7 %collective-permute-start = (bf16[1,512,384]{2,1,0:T(8,128)(2,1)S(1)}, bf16[1,512,384]{2,1,0:T(8,128)(2,1)S(1)}, u32[]{:S(2)}, u32[]{:S(2)}) collective-permute-start(bf16[1,512,384]{2,1,0:T(8,128)(2,1)S(1)} %get-tuple-element.123), channel_id=1, source_target_pairs={{0,2},{1,3},{2,0},{3,1},{4,6},{5,7},{6,4},{7,5},{8,10},{9,11},{10,... | collective-permute-start | bytes 1179656 | tf_op jit(solution)/shard_map/ppermute | solution.py:1059
  7.0 33.2 %collective-permute-start.1 = (bf16[1,512,384]{2,1,0:T(8,128)(2,1)S(1)}, bf16[1,512,384]{2,1,0:T(8,128)(2,1)S(1)}, u32[]{:S(2)}, u32[]{:S(2)}) collective-permute-start(bf16[1,512,384]{2,1,0:T(8,128)(2,1)S(1)} %get-tuple-element.122), channel_id=1, source_target_pairs={{0,3},{1,2},{2,1},{3,0},{4,7},{5,6},{6,5},{7,4},{8,11},{9,10},{10,... | collective-permute-start | bytes 1179656 | tf_op jit(solution)/shard_map/ppermute | solution.py:1059
  8.3 1.2 copy-start
  8.3 2.0 copy-start.1
  8.3 2.0 copy-start.10
  8.3 2.0 copy-start.11
  8.5 21.0 %copy-start.7 = (bf16[2,512,384]{2,1,0:T(8,128)(2,1)}, bf16[2,512,384]{2,1,0:T(8,128)(2,1)S(1)}, u32[]{:S(2)}) copy-start(bf16[2,512,384]{2,1,0:T(8,128)(2,1)S(1)} %collective-permute-done.2.refs_5_.sib_x.refs_2_) | copy-start | bytes 2359300
  8.5 43.0 %collective-permute-start.5 = (bf16[2,512,384]{2,1,0:T(8,128)(2,1)S(1)}, bf16[2,512,384]{2,1,0:T(8,128)(2,1)S(1)}, u32[]{:S(2)}, u32[]{:S(2)}) collective-permute-start(bf16[2,512,384]{2,1,0:T(8,128)(2,1)S(1)} %get-tuple-element.118), channel_id=1, source_target_pairs={{0,1},{1,0},{2,3},{3,2},{4,5},{5,4},{6,7},{7,6},{8,9},{9,8},{10,11... | collective-permute-start | bytes 2359304 | tf_op jit(solution)/shard_map/ppermute | solution.py:1059
  29.5 10.0 %copy-start.3 = (bf16[2,1024,384]{2,1,0:T(8,128)(2,1)}, bf16[2,1024,384]{2,1,0:T(8,128)(2,1)S(1)}, u32[]{:S(2)}) copy-start(bf16[2,1024,384]{2,1,0:T(8,128)(2,1)S(1)} %get-tuple-element.90) | copy-start | bytes 4718596
  40.2 11.3 %copy-start.8 = (bf16[2,512,384]{2,1,0:T(8,128)(2,1)S(1)}, bf16[2,512,384]{2,1,0:T(8,128)(2,1)}, u32[]{:S(2)}) copy-start(bf16[2,512,384]{2,1,0:T(8,128)(2,1)} %copy-done.7) | copy-start | bytes 2359300
  40.2 11.3 %copy-start.12 = (bf16[384,1536]{1,0:T(8,128)(2,1)S(1)}, bf16[384,1536]{1,0:T(8,128)(2,1)}, u32[]{:S(2)}) copy-start(bf16[384,1536]{1,0:T(8,128)(2,1)} %fc1_w.1) | copy-start | bytes 3538948
  40.2 11.3 %copy-start.13 = (bf16[1536,384]{1,0:T(8,128)(2,1)S(1)}, bf16[1536,384]{1,0:T(8,128)(2,1)}, u32[]{:S(2)}) copy-start(bf16[1536,384]{1,0:T(8,128)(2,1)} %fc2_w.1) | copy-start | bytes 3538948
  40.2 11.3 %copy-start.14 = (bf16[384,384]{1,0:T(8,128)(2,1)S(1)}, bf16[384,384]{1,0:T(8,128)(2,1)}, u32[]{:S(2)}) copy-start(bf16[384,384]{1,0:T(8,128)(2,1)} %out_w.1) | copy-start | bytes 884740
  50.4 1.1 copy-start.5
  51.5 34.2 %copy-start.6 = (bf16[2,3,1024,128]{3,2,1,0:T(8,128)(2,1)S(1)}, bf16[2,3,1024,128]{3,2,1,0:T(8,128)(2,1)}, u32[]{:S(2)}) copy-start(bf16[2,3,1024,128]{3,2,1,0:T(8,128)(2,1)} %copy-done.5) | copy-start | bytes 4718596
  85.4 39.8 %collective-permute-start.6 = (bf16[2,512,384]{2,1,0:T(8,128)(2,1)S(1)}, bf16[2,512,384]{2,1,0:T(8,128)(2,1)S(1)}, u32[]{:S(2)}, u32[]{:S(2)}) collective-permute-start(bf16[2,512,384]{2,1,0:T(8,128)(2,1)S(1)} %get-tuple-element.81), channel_id=1, source_target_pairs={{0,1},{1,0},{2,3},{3,2},{4,5},{5,4},{6,7},{7,6},{8,9},{9,8},{10,11... | collective-permute-start | bytes 2359304 | tf_op jit(solution)/shard_map/ppermute | solution.py:1059
  131.0 43.6 %collective-permute-start.7 = (bf16[2,2,512,384]{3,2,1,0:T(8,128)(2,1)S(1)}, bf16[2,2,512,384]{3,2,1,0:T(8,128)(2,1)S(1)}, u32[]{:S(2)}, u32[]{:S(2)}) collective-permute-start(bf16[2,2,512,384]{3,2,1,0:T(8,128)(2,1)S(1)} %get-tuple-element.96), channel_id=1, source_target_pairs={{0,2},{1,3},{2,0},{3,1},{4,6},{5,7},{6,4},{7,5},{8,10},{9,11},{10,... | collective-permute-start | bytes 4718600 | tf_op jit(solution)/shard_map/ppermute | solution.py:1059
  132.3 37.2 %copy-start.4 = (bf16[2,1024,384]{2,1,0:T(8,128)(2,1)S(1)}, bf16[2,1024,384]{2,1,0:T(8,128)(2,1)}, u32[]{:S(2)}) copy-start(bf16[2,1024,384]{2,1,0:T(8,128)(2,1)} %copy-done.3) | copy-start | bytes 4718596
  169.5 5.1 %copy-start.9 = (bf16[2,512,384]{2,1,0:T(8,128)(2,1)S(1)}, bf16[2,512,384]{2,1,0:T(8,128)(2,1)}, u32[]{:S(2)}) copy-start(bf16[2,512,384]{2,1,0:T(8,128)(2,1)} %copy-done.7) | copy-start | bytes 2359300
  174.6 35.5 %copy-start.2 = (bf16[384,2304]{1,0:T(8,128)(2,1)S(1)}, bf16[384,2304]{1,0:T(8,128)(2,1)}, u32[]{:S(2)}) copy-start(bf16[384,2304]{1,0:T(8,128)(2,1)} %refs_3_.5) | copy-start | bytes 5308420
where the time goes:
time: 219 us
  Pallas kernels  204 us (93%)
  starting transfers between devices  5.97 us (3%)
  local copies, waits for them, and re-layouts  5.78 us (3%)
    pallas_call x2, Pallas kernels, attend_back(): call(functools.partial(attend_back_kernel, min(512, count), first, early,...  76.6 us
    pallas_call x1, Pallas kernels, local(): call(functools.partial(tail_kernel, direct, len(dx_got)), 'tail', (steps,...  35.5 us
    pallas_call x1, Pallas kernels, local(): call(functools.partial(patch_kernel, block_rows, hidden_width), 'patchwis...  33.8 us
    pallas_call x2, Pallas kernels, far(): call(functools.partial(far_kernel, piece, step, remote), 'far', (pairs,),...  20.1 us
    pallas_call x1, Pallas kernels, local(): call(functools.partial(near_kernel, piece), 'near', (steps, pairs), [scal...  19.1 us
    pallas_call x1, Pallas kernels, local(): call(functools.partial(final_kernel, direct), 'final', (), [whole(value.s...  8.15 us
    ppermute x8, starting transfers between devices, send(): return lax.ppermute(values, 'seq', pairs_list)  5.97 us
    pallas_call x1, Pallas kernels, local(): call(project_back_far_kernel, 'project_back_far', (steps, remote), [grad_...  5.79 us
  transfers between devices with their start and end apart: 8, of which 1 were waited for; matrix products, arithmetic and copies ran while one was open for 0% of the time, Pallas kernels for 55%

commit v1 on v0

--- a/solution.py
+++ b/solution.py
@@ -596,7 +596,7 @@
     for weight in weights:
         total += weight
         marks.append(total)
-    last = static_slots - (2 if first_pass else 1)
+    last = static_slots - 1
     marks = [min(int(mark * last / total + 0.5), last) for mark in marks]
 
     dq_s[...] = jnp.zeros_like(dq_s) if first_pass else dq_in[0, 0].T
@@ -799,12 +799,42 @@
         lax.fori_loop(1, self.peers, one, 0)
 
 
+def spread_leads(grads, step_of, table_rows):
+    count = grads.shape[0]
+    part = min(count, 512)
+    row = lax.broadcasted_iota(jnp.int32, (part, part), 0)
+    column = lane_index((part, part))
+    chosen = (row // 16 == column // 16) & (row % 16 == 12 + step_of(column % 16))
+    spread = jnp.where(chosen, 1.0, 0.0).astype(BF16)
+    leads = [
+        dot(grads[start : start + part, :LANES], spread, TN)[:table_rows]
+        for start in range(0, count, part)
+    ]
+    return jnp.concatenate(leads, axis=-1)
+
+
+def lead_grads(emb_ref, ada_ref, grads, leads, place, columns, gada_ref, gbada_ref, target):
+    table = emb_ref[...].astype(F32)
+    table_act = (table * jax.nn.sigmoid(table)).astype(BF16)
+    chosen = jnp.where(place, leads, 0.0).astype(BF16)
+    acts = dot(table_act, chosen, TN).astype(BF16)
+    gada_ref[:, target] = dot(acts, grads)
+    by_lead = dot(chosen, grads)
+    gbada_ref[:, target] = jnp.sum(by_lead, axis=0, keepdims=True)
+    high = by_lead.astype(BF16)
+    low = (by_lead - high.astype(F32)).astype(BF16)
+    return dot(high, ada_ref[:, columns], NT) + dot(low, ada_ref[:, columns], NT)
+
+
 def tail_kernel(direct, remote, *refs):
     give_ref, own_x, sib_x, mod_ref, lead_ref, gm_ref, dq_ref, dk_ref, dv_ref, w_ref = refs[:10]
     others = refs[10 : 10 + remote]
-    grad_ref, got_ref, full_ref, all_ref = refs[10 + remote : 14 + remote]
-    sums_s, other_s, got_s, sum_s, core_s, pieces_s, full_s, all_s = refs[14 + remote : 22 + remote]
-    core_sems, piece_sems, back_sems, all_sems, grad_sems, local_sem = refs[22 + remote :]
+    early_sums, emb_ref, ada_ref = refs[10 + remote : 13 + remote]
+    grad_ref, got_ref, full_ref, all_ref = refs[13 + remote : 17 + remote]
+    gada_ref, gbada_ref, gemb_ref = refs[17 + remote : 20 + remote]
+    refs = refs[20 + remote :]
+    sums_s, other_s, got_s, sum_s, core_s, pieces_s, full_s, all_s = refs[:8]
+    core_sems, piece_sems, back_sems, all_sems, grad_sems, local_sem = refs[8:]
     step, half = pl.program_id(0), pl.program_id(1)
     width = own_x.shape[2]
     core, me = direct.core(), direct.me()
@@ -903,6 +933,18 @@
         total = lax.fori_loop(1, direct.peers, add, sum_s[direct.rows(me)].astype(F32))
         full_s[core, direct.rows(me)] = total.astype(BF16)
         direct.each_peer(lambda shift: full_copy(shift, False).start())
+        grads = early_sums[...]
+        leads = spread_leads(grads, lambda row: row % 2, emb_ref.shape[0])
+        row = lane_index((1, grads.shape[0])) % 16
+        part = jnp.zeros(gemb_ref.shape, F32)
+        for index in range(4):
+            columns = slice((2 + index) * width, (3 + index) * width)
+            target = slice(index * width, (index + 1) * width)
+            place = row // 2 == index
+            part += lead_grads(
+                emb_ref, ada_ref, grads, leads, place, columns, gada_ref, gbada_ref, target
+            )
+        gemb_ref[...] = part
 
         def arrived(shift):
             full_copy(shift, False).wait_send()
@@ -951,24 +993,11 @@
     return at
 
 
-def spread_leads(grads, step_of, table_rows):
-    count = grads.shape[0]
-    part = min(count, 512)
-    row = lax.broadcasted_iota(jnp.int32, (part, part), 0)
-    column = lane_index((part, part))
-    chosen = (row // 16 == column // 16) & (row % 16 == 12 + step_of(column % 16))
-    spread = jnp.where(chosen, 1.0, 0.0).astype(BF16)
-    leads = [
-        dot(grads[start : start + part, :LANES], spread, TN)[:table_rows]
-        for start in range(0, count, part)
-    ]
-    return jnp.concatenate(leads, axis=-1)
-
-
 def final_kernel(direct, *refs):
-    early_sums, late_sums, emb_ref, ada_ref, late_ref, own_ref, got_ref = refs[:7]
-    grad_out, gemb_ref, gada_out, gbada_ref, gqkv_out = refs[7:12]
-    gada_s, gqkv_s, late_s, own_s, got_s, sems = refs[12:]
+    late_sums, emb_ref, ada_ref, gada_part, gbada_part, gemb_part = refs[:6]
+    late_ref, own_ref, got_ref = refs[6:9]
+    grad_out, gemb_ref, gada_out, gbada_ref, gqkv_out = refs[9:14]
+    gada_s, gbada_s, gqkv_s, late_s, own_s, got_s, sems = refs[14:]
     size = emb_ref.shape[1]
     mine = first_step(2)
     pairs = [(late_ref, late_s), (own_ref, own_s), (got_ref, got_s)]
@@ -989,6 +1018,7 @@
         group, inside = divmod(row, direct.half)
         return group, inside, direct.half - inside
 
+    start(gada_part, gada_out.at[:, pl.ds(2 * size, 4 * size)])
     columns = gqkv_s.shape[1] // LANES
     reads[0].wait()
     unstack(halved, late_s, [(gqkv_s, 0, block * LANES) for block in range(columns)], size)
@@ -1002,25 +1032,7 @@
     table = emb_ref[...].astype(F32)
     gate = jax.nn.sigmoid(table)
     slope = gate * (1.0 + table * (1.0 - gate))
-    table_act = (table * gate).astype(BF16)
-    total = jnp.zeros((table_rows, size), F32)
-
-    def one_piece(grads, leads, place, first):
-        chosen = jnp.where(place, leads, 0.0).astype(BF16)
-        acts = dot(table_act, chosen, TN).astype(BF16)
-        where = slice(first, first + grads.shape[1])
-        gada_s[:, where] = dot(acts, grads)
-        by_lead = dot(chosen, grads)
-        gbada_ref[where] = jnp.sum(by_lead, axis=0)
-        high = by_lead.astype(BF16)
-        low = (by_lead - high.astype(F32)).astype(BF16)
-        return dot(high, ada_ref[:, where], NT) + dot(low, ada_ref[:, where], NT)
-
-    grads = early_sums[...]
-    leads = spread_leads(grads, lambda row: row % 2, table_rows)
-    row = lane_index((1, grads.shape[0])) % 16
-    for index in range(4):
-        total += one_piece(grads, leads, row // 2 == index, (2 + index) * size)
+    total = gemb_part[...]
     grads = late_sums[...]
     parts = size // LANES
     leads = spread_leads(grads, lambda row: (row // parts) % 2, table_rows)
@@ -1028,9 +1040,14 @@
     for index in range(2):
         for part in range(parts):
             place = (row // (2 * parts) == index) & (row % parts == part)
-            total += one_piece(grads, leads, place, index * size + part * LANES)
+            columns = slice(index * size + part * LANES, index * size + (part + 1) * LANES)
+            total += lead_grads(
+                emb_ref, ada_ref, grads, leads, place, columns, gada_s, gbada_s, columns
+            )
     gemb_ref[...] = total * slope
-    start(gada_s, gada_out)
+    start(gada_s, gada_out.at[:, pl.ds(0, 2 * size)])
+    gbada_ref[: 2 * size] = gbada_s[0]
+    gbada_ref[2 * size :] = gbada_part[0]
     for copy in copies:
         copy.wait()
 
@@ -1293,7 +1310,8 @@
     direct = Direct(mesh_shape, columns * width // 16)
     full_shape = (2, direct.padded, LANES)
     late_all_shape = (2, direct.peers, 16, LANES)
-    grad_own, grad_got, late_sum, late_all = call(
+    early_all = early_all.reshape(-1, width)
+    grad_own, grad_got, late_sum, late_all, *early_parts = call(
         functools.partial(tail_kernel, direct, len(dx_got)),
         "tail",
         (steps, 2),
@@ -1301,13 +1319,18 @@
         + [patch_block]
         + [grad_block] * 3
         + [whole(w_qkv.shape)]
-        + [patch_block] * len(dx_got),
-        [step_block, hbm, hbm, hbm],
+        + [patch_block] * len(dx_got)
+        + [whole(early_all.shape), whole(emb_table.shape), whole(w_ada.shape)],
+        [step_block, hbm, hbm, hbm]
+        + [whole((width, 4 * width)), whole((1, 4 * width)), whole(emb_table.shape)],
         [
             jax.ShapeDtypeStruct((steps, patches, width), BF16),
             jax.ShapeDtypeStruct((steps, patches, width), BF16),
             jax.ShapeDtypeStruct(full_shape, BF16),
             jax.ShapeDtypeStruct(late_all_shape, BF16),
+            jax.ShapeDtypeStruct((width, 4 * width), F32),
+            jax.ShapeDtypeStruct((1, 4 * width), F32),
+            jax.ShapeDtypeStruct(emb_table.shape, F32),
         ],
         [
             pltpu.VMEM((16, LANES), F32),
@@ -1339,11 +1362,13 @@
         dv,
         w_qkv,
         *dx_got,
+        early_all,
+        emb_table,
+        w_ada,
     )
 
-    early_all = early_all.reshape(-1, width)
     late_all = late_all.reshape(-1, LANES)
-    small = [early_all, late_all, emb_table, w_ada]
+    small = [late_all, emb_table, w_ada, *early_parts]
     large = [late_sum, grad_own, grad_got]
     out_shapes = [(slots * items, patches, width), emb_table.shape, w_ada.shape, b_ada.shape, w_qkv.shape]
     grad_inputs, g_emb, g_ada, g_bada, g_qkv = call(
@@ -1356,10 +1381,10 @@
             jax.ShapeDtypeStruct(shape, F32 if index else BF16)
             for index, shape in enumerate(out_shapes)
         ],
-        [pltpu.VMEM(w.shape, F32) for w in (w_ada, w_qkv)]
+        [pltpu.VMEM(shape, F32) for shape in ((width, 2 * width), (1, 2 * width), w_qkv.shape)]
         + [pltpu.VMEM(value.shape, BF16) for value in large]
-        + [pltpu.SemaphoreType.DMA((7,))],
-        flops=2 * early_all.shape[0] * width * 6 * width,
+        + [pltpu.SemaphoreType.DMA((8,))],
+        flops=2 * late_all.shape[0] * width * 6 * width,
         moved=6 * w_ada.size,
     )(*small, *large)
     return (

time: 219 us -> 232 us (1.059)
  local copies, waits for them, and re-layouts: 5.78 us -> 18.6 us
    unnamed x36 -> x52, local copies, waits for them, and re-layouts: 2.92 us -> 15.8 us
    pallas_call x1, Pallas kernels: 8.15 us -> 4.67 us  [local(): call(functools.partial(final_kernel, direct), 'final', (), [whole(value.s...]
  transfers between devices with their start and end apart: 8 -> 8, of which waited for: 1 -> 1; matrix products, arithmetic and copies ran while one was open for 0% -> 0% of each run, Pallas kernels for 55% -> 53%
where the time goes in v1:
time: 232 us
  Pallas kernels  204 us (88%)
  local copies, waits for them, and re-layouts  18.6 us (8%)
  starting transfers between devices  5.9 us (3%)
    pallas_call x2, Pallas kernels, attend_back(): call(functools.partial(attend_back_kernel, min(512, count), first, early,...  78.5 us
    pallas_call x1, Pallas kernels, local(): call(functools.partial(tail_kernel, direct, len(dx_got)), 'tail', (steps,...  35.8 us
    pallas_call x1, Pallas kernels, local(): call(functools.partial(patch_kernel, block_rows, hidden_width), 'patchwis...  35.4 us
    pallas_call x2, Pallas kernels, far(): call(functools.partial(far_kernel, piece, step, remote), 'far', (pairs,),...  19.9 us
    pallas_call x1, Pallas kernels, local(): call(functools.partial(near_kernel, piece), 'near', (steps, pairs), [scal...  19.1 us
    unnamed x52, local copies, waits for them, and re-layouts  15.8 us
    ppermute x8, starting transfers between devices, send(): return lax.ppermute(values, 'seq', pairs_list)  5.9 us
    pallas_call x1, Pallas kernels, local(): call(project_back_far_kernel, 'project_back_far', (steps, remote), [grad_...  5.75 us
  transfers between devices with their start and end apart: 8, of which 1 were waited for; matrix products, arithmetic and copies ran while one was open for 0% of the time, Pallas kernels for 53%

profile of v1, /device:TPU:27, one launch (start us, length us, event | category | flops | bytes accessed | tf_op | source)
XLA Modules:
  0.0 231.7 jit_solution(15766072015927296461)
XLA Ops:
  0.7 0.0 copy-start.23
  0.7 2.5 %dynamic-slice_bitcast_fusion.2 = (bf16[2,512,384]{2,1,0:T(8,128)(2,1)}, bf16[2,512,384]{2,1,0:T(8,128)(2,1)S(1)}) fusion(bf16[2,2,512,384]{3,2,1,0:T(8,128)(2,1)} %bitcast.38, s32[]{:T(128)S(6)} %select_n.10, s32[]{:T(128)S(6)} %select_n.9), kind=kLoop, calls=%fused_computation.2 | loop fusion | bytes 3145736 | tf_op jit(solution)/shard_map/jit(dynamic_index_in_dim)/squeeze | solution.py:1081
  3.2 0.7 collective-permute-start.2
  3.9 0.0 copy-done.23
  3.9 0.0 copy-start.25
  3.9 0.2 dynamic-slice_bitcast_fusion.4
  4.0 1.3 collective-permute-start.3
  5.3 0.4 collective-permute-start.4
  5.8 1.2 collective-permute-start
  7.0 0.6 collective-permute-start.1
  7.6 0.0 copy-done.25
  8.3 0.0 copy-done.24
  8.3 0.0 copy-start
  8.3 0.0 copy-start.1
  8.3 0.0 copy-start.10
  8.3 0.0 copy-start.11
  8.3 0.2 dynamic-slice_bitcast_fusion
  8.5 0.0 collective-permute-done.2.refs_5_.sib_x.refs_2_
  8.5 0.1 collective-permute-start.5
  8.6 0.8 copy-done
  9.4 0.6 copy-done.1
  10.0 0.0 copy-done.10
  10.0 0.0 copy-done.11
  10.0 19.1 %near.1 = (f32[16,2304]{1,0:T(8,128)S(1)}, bf16[2,1024,384]{2,1,0:T(8,128)(2,1)S(1)}, bf16[2,3,1024,128]{3,2,1,0:T(8,128)(2,1)S(1)}, bf16[2,3,1024,128]{3,2,1,0:...) custom-call(s32[1,4]{1,0:T(1,128)S(1)} %copy-done.11, ...), custom_call_target="tpu_custom_call" | custom-call | flops 8254390272 | tf_op jit(solution)/shard_map/near/pallas_call | solution.py:1106
  29.1 0.0 collective-permute-done.3.refs_0_
  29.2 0.0 collective-permute-done.4.refs_1_
  29.2 10.0 %far.2 = (bf16[2,1024,384]{2,1,0:T(8,128)(2,1)S(1)}, bf16[2,3,1024,128]{3,2,1,0:T(8,128)(2,1)S(1)}, bf16[2,3,1024,128]{3,2,1,0:T(8,128)(2,1)S(1)}, f32[2,3,1024,...) custom-call(bf16[1,512,384]{2,1,0:T(8,128)(2,1)S(1)} %collective-permute-done.3.refs_0_, ...), custom_call_target="tpu_custom_call" | custom-call | flops 3221225472 | tf_op jit(solution)/shard_map/far/pallas_call | solution.py:1139
  39.2 0.0 collective-permute-done.refs_0_
  39.2 1.1 collective-permute-done.1.refs_1_
  40.2 9.9 %far.3 = (bf16[2,1024,384]{2,1,0:T(8,128)(2,1)S(1)}, bf16[2,3,1024,128]{3,2,1,0:T(8,128)(2,1)S(1)}, bf16[2,3,1024,128]{3,2,1,0:T(8,128)(2,1)S(1)}, f32[2,3,1024,...) custom-call(bf16[1,512,384]{2,1,0:T(8,128)(2,1)S(1)} %collective-per, ...), custom_call_target="tpu_custom_call", output_to_operand_aliasing={{0}: (8, {}), {1}: (9, {}), {2}: (10, {}), {3}: (11, {}), {... | custom-call | flops 3221225472 | tf_op jit(solution)/shard_map/far/pallas_call | solution.py:1139
  50.2 0.0 copy-start.2
  50.2 1.7 copy-done.2
  51.8 1.1 copy-done.6
  53.0 1.1 copy-done.8
  54.1 0.0 collective-permute-done.5.sib_ct
  54.1 0.0 copy-done.12
  54.1 0.0 copy-done.13
  54.1 0.0 copy-done.14
  54.2 0.0 copy-start.3
  54.2 3.0 %copy-done.3 = f32[2,3,1024,128]{3,2,1,0:T(8,128)S(1)} copy-done((f32[2,3,1024,128]{3,2,1,0:T(8,128)S(1)}, f32[2,3,1024,128]{3,2,1,0:T(8,128)}, u32[]{:S(2)}) %copy-start.3) | copy-done | bytes 3145752
  57.2 35.4 %patchwise.1 = (bf16[2,512,384]{2,1,0:T(8,128)(2,1)S(1)}, bf16[2,512,384]{2,1,0:T(8,128)(2,1)}, f32[2,2,512,384]{3,2,1,0:T(8,128)S(1)}, bf16[2,3,2,1024,128]{4,3...) custom-call(s32[1]{0:T(128)S(6)} %copy.32.counts_ref, ...), custom_call_target="tpu_custom_call" | custom-call | flops 16307453952 | bytes 15728640 | tf_op jit(solution)/shard_map/patchwise/pallas_call | solution.py:1170
  92.6 1.1 copy-done.15
  93.7 1.0 copy-done.17
  94.7 0.9 copy-done.19
  95.6 0.3 collective-permute-start.6
  95.9 0.0 copy-done.4
  95.9 0.0 copy-done.7
  95.9 0.0 copy-done.9
  95.9 1.4 copy-done.16
  97.3 1.3 copy-done.18
  98.5 39.2 %attend_back_far.1 = (f32[2,3,1024,128]{3,2,1,0:T(8,128)S(1)}, bf16[2,3,1024,128]{3,2,1,0:T(8,128)(2,1)S(1)}, bf16[2,3,1024,128]{3,2,1,0:T(8,128)(2,1)S(1)}, bf1...) custom-call(bf16[2,3,2,1024,128]{4,3,2,1,0:T(8,128)(2,1)S(1)} %get-tuple-element.72.refs_0_,, ...), custom_call_target="tpu_custom_call" | custom-call | flops 16106127360 | tf_op jit(solution)/shard_map/attend_back_far/pallas_call | solution.py:1254
  137.7 0.0 copy-start.21
  137.7 1.7 copy-done.21
  139.4 0.0 collective-permute-done.6.got_ref
  139.4 0.0 copy-done.20
  139.4 5.8 %project_back_far.1 = (bf16[2,2,512,384]{3,2,1,0:T(8,128)(2,1)S(1)}, f32[384,768]{1,0:T(8,128)S(1)}, bf16[4,512,384]{2,1,0:T(8,128)(2,1)}) custom-call(bf16[2,3,1024,128]{3,2,1,0:T(8,128)(2,1)S(1)} %get-tuple-element.80.dk_ref, bf16[2,3,1024,128]{3,2,1,0:T(8,128)(2,1)S(1)} %get-tuple-element.81.dv_ref, bf16[2,2,512,384]{3,2,1,0:T(8,128)(2,1)S(1)} %bitcast.32, ...), custom_call_target="tpu_custom_call" | custom-call | flops 2415919104 | bytes 6291456 | tf_op jit(solution)/shard_map/project_back_far/pallas_call | solution.py:1273
  145.2 1.3 collective-permute-start.7
  146.5 0.0 copy-done.5
  146.5 0.0 copy-done.22
  146.5 39.4 %attend_back_near.1 = (bf16[2,3,1024,128]{3,2,1,0:T(8,128)(2,1)S(1)}, bf16[2,3,1024,128]{3,2,1,0:T(8,128)(2,1)S(1)}, bf16[2,3,1024,128]{3,2,1,0:T(8,128)(2,1)S(1...) custom-call(bf16[2,3,2,1024,128]{4,3,2,1,0:T(8,128)(2,1)S(1)} %copy-done.5, ...), custom_call_target="tpu_custom_call" | custom-call | flops 16106127360 | tf_op jit(solution)/shard_map/attend_back_near/pallas_call | solution.py:1254
  185.8 5.1 %weight_back.1 = (bf16[9,384,128]{2,1,0:T(8,128)(2,1)S(1)}, f32[384,1536]{1,0:T(8,128)}, f32[1536,384]{1,0:T(8,128)}, f32[384,384]{1,0:T(8,128)}) custom-call(bf16[2,3,1024,128]{3,2,1,0:T(8,128)(2,1)S(1)} %get-tuple-element.89.refs_0_.refs_6_, bf16[2,3,1024,128]{3,2,1,0:T(8,128)(2,1)S(1)} %get-tuple-element.90.refs_1_.refs_7_, ...), custom_call_target="tpu_custom_call" | custom-call | flops 1811939328 | bytes 6291456 | tf_op jit(solution)/shard_map/weight_back/pallas_call | solution.py:1294
  190.9 0.0 collective-permute-done.7.refs_10_
  190.9 35.8 %tail.1 = (bf16[2,512,384]{2,1,0:T(8,128)(2,1)S(1)}, bf16[2,512,384]{2,1,0:T(8,128)(2,1)S(1)}, bf16[2,1792,128]{2,1,0:T(8,128)(2,1)S(1)}, bf16[2,16,16,128]{3,2,...) custom-call(bf16[2,1728,128]{2,1,0:T(8,128)(2,1)S(1)} %bitcast.33, ...), custom_call_target="tpu_custom_call" | custom-call | flops 1811939328 | tf_op jit(solution)/shard_map/tail/pallas_call | solution.py:1314
  226.8 4.7 %final.1 = (bf16[4,512,384]{2,1,0:T(8,128)(2,1)}, f32[16,384]{1,0:T(8,128)}, f32[384,2304]{1,0:T(8,128)}, f32[2304]{0:T(1024)}, f32[384,1152]{1,0:T(8,128)}) custom-call(bf16[512,128]{1,0:T(8,128)(2,1)S(1)} %bitcast.35, bf16[16,384]{1,0:T(8,128)(2,1)S(1)} %copy-done.10, bf16[384,2304]{1,0:T(8,128)(2,1)S(1)} %copy-done.1, ...), custom_call_target="tpu_custom_call" | custom-call | flops 905969664 | bytes 5308416 | tf_op jit(solution)/shard_map/final/pallas_call | solution.py:1374
  (18 shorter events, 0.0 us)
Async XLA Ops:
  0.7 3.2 %copy-start.23 = (bf16[4,1,512,384]{3,2,1,0:T(8,128)(2,1)S(1)}, bf16[4,1,512,384]{3,2,1,0:T(8,128)(2,1)}, u32[]{:S(2)}) copy-start(bf16[4,1,512,384]{3,2,1,0:T(8,128)(2,1)} %param.11) | copy-start | bytes 4718596
  3.2 5.3 %collective-permute-start.2 = (bf16[2,512,384]{2,1,0:T(8,128)(2,1)}, bf16[2,512,384]{2,1,0:T(8,128)(2,1)S(1)}, u32[]{:S(2)}, u32[]{:S(2)}) collective-permute-start(bf16[2,512,384]{2,1,0:T(8,128)(2,1)} %get-tuple-element.130), channel_id=1, source_target_pairs={{0,1},{1,0},{2,3},{3,2},{4,5},{5,4},{6,7},{7,6},{8,9},{9,8},{10,11... | collective-permute-start | bytes 2359304 | tf_op jit(solution)/shard_map/ppermute | solution.py:1076
  3.9 3.7 %copy-start.25 = (bf16[2304]{0:T(1024)(128)(2,1)S(1)}, bf16[2304]{0:T(1024)(128)(2,1)}, u32[]{:S(2)}) copy-start(bf16[2304]{0:T(1024)(128)(2,1)} %param.17) | copy-start | bytes 13828
  3.9 4.4 %copy-start.24 = (bf16[4,1,512,384]{3,2,1,0:T(8,128)(2,1)S(1)}, bf16[4,1,512,384]{3,2,1,0:T(8,128)(2,1)}, u32[]{:S(2)}) copy-start(bf16[4,1,512,384]{3,2,1,0:T(8,128)(2,1)} %param.12) | copy-start | bytes 4718596
  4.0 25.1 %collective-permute-start.3 = (bf16[1,512,384]{2,1,0:T(8,128)(2,1)S(1)}, bf16[1,512,384]{2,1,0:T(8,128)(2,1)S(1)}, u32[]{:S(2)}, u32[]{:S(2)}) collective-permute-start(bf16[1,512,384]{2,1,0:T(8,128)(2,1)S(1)} %get-tuple-element.127), channel_id=1, source_target_pairs={{0,2},{1,3},{2,0},{3,1},{4,6},{5,7},{6,4},{7,5},{8,10},{9,11},{10,... | collective-permute-start | bytes 1179656 | tf_op jit(solution)/shard_map/ppermute | solution.py:1076
  5.3 23.8 %collective-permute-start.4 = (bf16[1,512,384]{2,1,0:T(8,128)(2,1)S(1)}, bf16[1,512,384]{2,1,0:T(8,128)(2,1)S(1)}, u32[]{:S(2)}, u32[]{:S(2)}) collective-permute-start(bf16[1,512,384]{2,1,0:T(8,128)(2,1)S(1)} %get-tuple-element.126), channel_id=1, source_target_pairs={{0,3},{1,2},{2,1},{3,0},{4,7},{5,6},{6,5},{7,4},{8,11},{9,10},{10,... | collective-permute-start | bytes 1179656 | tf_op jit(solution)/shard_map/ppermute | solution.py:1076
  5.8 33.4 %collective-permute-start = (bf16[1,512,384]{2,1,0:T(8,128)(2,1)S(1)}, bf16[1,512,384]{2,1,0:T(8,128)(2,1)S(1)}, u32[]{:S(2)}, u32[]{:S(2)}) collective-permute-start(bf16[1,512,384]{2,1,0:T(8,128)(2,1)S(1)} %get-tuple-element.129), channel_id=1, source_target_pairs={{0,2},{1,3},{2,0},{3,1},{4,6},{5,7},{6,4},{7,5},{8,10},{9,11},{10,... | collective-permute-start | bytes 1179656 | tf_op jit(solution)/shard_map/ppermute | solution.py:1076
  7.0 33.2 %collective-permute-start.1 = (bf16[1,512,384]{2,1,0:T(8,128)(2,1)S(1)}, bf16[1,512,384]{2,1,0:T(8,128)(2,1)S(1)}, u32[]{:S(2)}, u32[]{:S(2)}) collective-permute-start(bf16[1,512,384]{2,1,0:T(8,128)(2,1)S(1)} %get-tuple-element.128), channel_id=1, source_target_pairs={{0,3},{1,2},{2,1},{3,0},{4,7},{5,6},{6,5},{7,4},{8,11},{9,10},{10,... | collective-permute-start | bytes 1179656 | tf_op jit(solution)/shard_map/ppermute | solution.py:1076
  8.3 1.2 copy-start
  8.3 1.7 copy-start.1
  8.3 1.7 copy-start.10
  8.3 1.7 copy-start.11
  8.5 45.6 %collective-permute-start.5 = (bf16[2,512,384]{2,1,0:T(8,128)(2,1)S(1)}, bf16[2,512,384]{2,1,0:T(8,128)(2,1)S(1)}, u32[]{:S(2)}, u32[]{:S(2)}) collective-permute-start(bf16[2,512,384]{2,1,0:T(8,128)(2,1)S(1)} %get-tuple-element.124), channel_id=1, source_target_pairs={{0,1},{1,0},{2,3},{3,2},{4,5},{5,4},{6,7},{7,6},{8,9},{9,8},{10,11... | collective-permute-start | bytes 2359304 | tf_op jit(solution)/shard_map/ppermute | solution.py:1076
  40.2 13.9 %copy-start.12 = (bf16[384,1536]{1,0:T(8,128)(2,1)S(1)}, bf16[384,1536]{1,0:T(8,128)(2,1)}, u32[]{:S(2)}) copy-start(bf16[384,1536]{1,0:T(8,128)(2,1)} %fc1_w.1) | copy-start | bytes 3538948
  40.2 13.9 %copy-start.13 = (bf16[1536,384]{1,0:T(8,128)(2,1)S(1)}, bf16[1536,384]{1,0:T(8,128)(2,1)}, u32[]{:S(2)}) copy-start(bf16[1536,384]{1,0:T(8,128)(2,1)} %fc2_w.1) | copy-start | bytes 3538948
  40.2 13.9 %copy-start.14 = (bf16[384,384]{1,0:T(8,128)(2,1)S(1)}, bf16[384,384]{1,0:T(8,128)(2,1)}, u32[]{:S(2)}) copy-start(bf16[384,384]{1,0:T(8,128)(2,1)} %out_w.1) | copy-start | bytes 884740
  50.2 1.7 copy-start.2
  51.8 1.1 copy-start.6
  53.0 1.1 copy-start.8
  54.1 41.8 %copy-start.4 = (bf16[2,3,2,1024,128]{4,3,2,1,0:T(8,128)(2,1)}, bf16[2,3,2,1024,128]{4,3,2,1,0:T(8,128)(2,1)S(1)}, u32[]{:S(2)}) copy-start(bf16[2,3,2,1024,128]{4,3,2,1,0:T(8,128)(2,1)S(1)} %get-tuple-element.72.refs_0_) | copy-start | bytes 9437188
  54.2 3.0 %copy-start.3 = (f32[2,3,1024,128]{3,2,1,0:T(8,128)S(1)}, f32[2,3,1024,128]{3,2,1,0:T(8,128)}, u32[]{:S(2)}) copy-start(f32[2,3,1024,128]{3,2,1,0:T(8,128)} %copy-done.2) | copy-start | bytes 9437188
  57.2 38.7 %copy-start.7 = (bf16[2,3,1024,128]{3,2,1,0:T(8,128)(2,1)S(1)}, bf16[2,3,1024,128]{3,2,1,0:T(8,128)(2,1)}, u32[]{:S(2)}) copy-start(bf16[2,3,1024,128]{3,2,1,0:T(8,128)(2,1)} %copy-done.6) | copy-start | bytes 4718596
  57.2 38.7 %copy-start.9 = (bf16[2,3,1024,128]{3,2,1,0:T(8,128)(2,1)S(1)}, bf16[2,3,1024,128]{3,2,1,0:T(8,128)(2,1)}, u32[]{:S(2)}) copy-start(bf16[2,3,1024,128]{3,2,1,0:T(8,128)(2,1)} %copy-done.8) | copy-start | bytes 4718596
  92.6 1.1 copy-start.15
  93.7 1.0 copy-start.17
  94.7 0.9 copy-start.19
  95.6 43.8 %collective-permute-start.6 = (bf16[2,512,384]{2,1,0:T(8,128)(2,1)}, bf16[2,512,384]{2,1,0:T(8,128)(2,1)S(1)}, u32[]{:S(2)}, u32[]{:S(2)}) collective-permute-start(bf16[2,512,384]{2,1,0:T(8,128)(2,1)} %get-tuple-element.84), channel_id=1, source_target_pairs={{0,1},{1,0},{2,3},{3,2},{4,5},{5,4},{6,7},{7,6},{8,9},{9,8},{10,11... | collective-permute-start | bytes 2359304 | tf_op jit(solution)/shard_map/ppermute | solution.py:1076
  95.9 1.4 copy-start.16
  97.3 1.3 copy-start.18
  98.5 40.9 %copy-start.20 = (bf16[2,512,384]{2,1,0:T(8,128)(2,1)S(1)}, bf16[2,512,384]{2,1,0:T(8,128)(2,1)}, u32[]{:S(2)}) copy-start(bf16[2,512,384]{2,1,0:T(8,128)(2,1)} %copy-done.19) | copy-start | bytes 2359300
  137.7 1.7 copy-start.21
  139.4 7.1 %copy-start.5 = (bf16[2,3,2,1024,128]{4,3,2,1,0:T(8,128)(2,1)S(1)}, bf16[2,3,2,1024,128]{4,3,2,1,0:T(8,128)(2,1)}, u32[]{:S(2)}) copy-start(bf16[2,3,2,1024,128]{4,3,2,1,0:T(8,128)(2,1)} %copy-done.4) | copy-start | bytes 9437188
  139.4 7.1 %copy-start.22 = (f32[2,3,1024,128]{3,2,1,0:T(8,128)S(1)}, f32[2,3,1024,128]{3,2,1,0:T(8,128)}, u32[]{:S(2)}) copy-start(f32[2,3,1024,128]{3,2,1,0:T(8,128)} %copy-done.21) | copy-start | bytes 9437188
  145.2 45.8 %collective-permute-start.7 = (bf16[2,2,512,384]{3,2,1,0:T(8,128)(2,1)S(1)}, bf16[2,2,512,384]{3,2,1,0:T(8,128)(2,1)S(1)}, u32[]{:S(2)}, u32[]{:S(2)}) collective-permute-start(bf16[2,2,512,384]{3,2,1,0:T(8,128)(2,1)S(1)} %get-tuple-element.98), channel_id=1, source_target_pairs={{0,2},{1,3},{2,0},{3,1},{4,6},{5,7},{6,4},{7,5},{8,10},{9,11},{10,... | collective-permute-start | bytes 4718600 | tf_op jit(solution)/shard_map/ppermute | solution.py:1076

commit v2 on v1

--- a/solution.py
+++ b/solution.py
@@ -16,7 +16,8 @@
 TN = (((0,), (0,)), ((), ()))
 F32 = jnp.float32
 BF16 = jnp.bfloat16
-VMEM_BYTES = 24 * 1024 * 1024
+MIB = 1024 * 1024
+GRANTS = {"patchwise": 20, "weight_back": 18}
 
 
 def dot(a, b, dims=NN):
@@ -48,7 +49,7 @@
         input_output_aliases=aliases or {},
         cost_estimate=pl.CostEstimate(flops=flops, bytes_accessed=moved, transcendentals=exps),
         compiler_params=pltpu.CompilerParams(
-            vmem_limit_bytes=VMEM_BYTES,
+            vmem_limit_bytes=GRANTS.get(name, 16) * MIB,
             collective_id=collective,
             has_side_effects=collective is not None,
         ),
@@ -596,7 +597,7 @@
     for weight in weights:
         total += weight
         marks.append(total)
-    last = static_slots - 1
+    last = static_slots - (2 if first_pass else 1)
     marks = [min(int(mark * last / total + 0.5), last) for mark in marks]
 
     dq_s[...] = jnp.zeros_like(dq_s) if first_pass else dq_in[0, 0].T

time: 232 us -> 218 us (0.940)
  local copies, waits for them, and re-layouts: 18.6 us -> 7.77 us
  Pallas kernels: 204 us -> 201 us
    unnamed x52 -> x32, local copies, waits for them, and re-layouts: 15.8 us -> 4.91 us
  transfers between devices with their start and end apart: 8 -> 8, of which waited for: 1 -> 1; matrix products, arithmetic and copies ran while one was open for 0% -> 0% of each run, Pallas kernels for 53% -> 56%
where the time goes in v2:
time: 218 us
  Pallas kernels  201 us (92%)
  local copies, waits for them, and re-layouts  7.77 us (4%)
  starting transfers between devices  5.96 us (3%)
    pallas_call x2, Pallas kernels, attend_back(): call(functools.partial(attend_back_kernel, min(512, count), first, early,...  77 us
    pallas_call x1, Pallas kernels, local(): call(functools.partial(tail_kernel, direct, len(dx_got)), 'tail', (steps,...  35.7 us
    pallas_call x1, Pallas kernels, local(): call(functools.partial(patch_kernel, block_rows, hidden_width), 'patchwis...  34.2 us
    pallas_call x2, Pallas kernels, far(): call(functools.partial(far_kernel, piece, step, remote), 'far', (pairs,),...  19.9 us
    pallas_call x1, Pallas kernels, local(): call(functools.partial(near_kernel, piece), 'near', (steps, pairs), [scal...  19.1 us
    ppermute x8, starting transfers between devices, send(): return lax.ppermute(values, 'seq', pairs_list)  5.96 us
    pallas_call x1, Pallas kernels, local(): call(project_back_far_kernel, 'project_back_far', (steps, remote), [grad_...  5.75 us
    pallas_call x1, Pallas kernels, local(): call(functools.partial(weight_back_kernel, early), 'weight_back', (steps,...  5.08 us
  transfers between devices with their start and end apart: 8, of which 1 were waited for; matrix products, arithmetic and copies ran while one was open for 0% of the time, Pallas kernels for 56%

profile of v2, /device:TPU:27, one launch (start us, length us, event | category | flops | bytes accessed | tf_op | source)
XLA Modules:
  0.0 218.0 jit_solution(1194436085222329374)
XLA Ops:
  0.7 0.0 copy-start.13
  0.7 2.5 %dynamic-slice_bitcast_fusion.2 = (bf16[2,512,384]{2,1,0:T(8,128)(2,1)}, bf16[2,512,384]{2,1,0:T(8,128)(2,1)S(1)}) fusion(bf16[2,2,512,384]{3,2,1,0:T(8,128)(2,1)} %bitcast.38, s32[]{:T(128)S(6)} %select_n.10, s32[]{:T(128)S(6)} %select_n.9), kind=kLoop, calls=%fused_computation.2 | loop fusion | bytes 3145736 | tf_op jit(solution)/shard_map/jit(dynamic_index_in_dim)/squeeze | solution.py:1082
  3.2 0.7 collective-permute-start.2
  3.9 0.0 copy-done.13
  3.9 0.0 copy-start.15
  3.9 0.0 copy-start.14
  3.9 0.2 dynamic-slice_bitcast_fusion.4
  4.0 1.3 collective-permute-start.3
  5.3 0.4 collective-permute-start.4
  5.8 1.2 collective-permute-start
  7.0 0.6 collective-permute-start.1
  7.6 0.0 copy-done.15
  8.3 0.0 copy-done.14
  8.3 0.0 copy-start
  8.3 0.0 copy-start.1
  8.3 0.0 copy-start.8
  8.3 0.0 copy-start.9
  8.3 0.2 dynamic-slice_bitcast_fusion
  8.5 0.0 collective-permute-done.2.refs_5_.sib_x.refs_2_
  8.5 0.1 collective-permute-start.5
  8.6 0.8 copy-done
  9.4 0.6 copy-done.1
  10.0 0.0 copy-done.8
  10.0 0.0 copy-done.9
  10.0 19.1 %near.1 = (f32[16,2304]{1,0:T(8,128)S(1)}, bf16[2,1024,384]{2,1,0:T(8,128)(2,1)S(1)}, bf16[2,3,1024,128]{3,2,1,0:T(8,128)(2,1)S(1)}, bf16[2,3,1024,128]{3,2,1,0:...) custom-call(s32[1,4]{1,0:T(1,128)S(1)} %copy-done.9, ...), custom_call_target="tpu_custom_call" | custom-call | flops 8254390272 | tf_op jit(solution)/shard_map/near/pallas_call | solution.py:1107
  29.1 0.0 collective-permute-done.3.refs_0_
  29.2 0.0 collective-permute-done.4.refs_1_
  29.2 10.0 %far.2 = (bf16[2,1024,384]{2,1,0:T(8,128)(2,1)S(1)}, bf16[2,3,1024,128]{3,2,1,0:T(8,128)(2,1)S(1)}, bf16[2,3,1024,128]{3,2,1,0:T(8,128)(2,1)S(1)}, f32[2,3,1024,...) custom-call(bf16[1,512,384]{2,1,0:T(8,128)(2,1)S(1)} %collective-permute-done.3.refs_0_, ...), custom_call_target="tpu_custom_call" | custom-call | flops 3221225472 | tf_op jit(solution)/shard_map/far/pallas_call | solution.py:1140
  39.2 0.0 collective-permute-done.refs_0_
  39.2 1.1 collective-permute-done.1.refs_1_
  40.2 0.0 copy-start.10
  40.2 0.0 copy-start.11
  40.2 0.0 copy-start.12
  40.2 10.0 %far.3 = (bf16[2,1024,384]{2,1,0:T(8,128)(2,1)S(1)}, bf16[2,3,1024,128]{3,2,1,0:T(8,128)(2,1)S(1)}, bf16[2,3,1024,128]{3,2,1,0:T(8,128)(2,1)S(1)}, f32[2,3,1024,...) custom-call(bf16[1,512,384]{2,1,0:T(8,128)(2,1)S(1)} %collective-per, ...), custom_call_target="tpu_custom_call", output_to_operand_aliasing={{0}: (8, {}), {1}: (9, {}), {2}: (10, {}), {3}: (11, {}), {... | custom-call | flops 3221225472 | tf_op jit(solution)/shard_map/far/pallas_call | solution.py:1140
  50.2 0.0 copy-start.2
  50.2 1.1 copy-done.2
  51.3 0.0 copy-start.4
  51.3 1.1 copy-done.4
  52.5 0.0 copy-start.6
  52.5 1.1 copy-done.6
  53.6 0.0 collective-permute-done.5.sib_ct
  53.6 0.0 copy-done.10
  53.6 0.0 copy-done.11
  53.6 0.0 copy-done.12
  53.6 0.0 copy-start.5
  53.7 0.0 copy-start.7
  53.7 34.2 %patchwise.1 = (bf16[2,512,384]{2,1,0:T(8,128)(2,1)S(1)}, bf16[2,512,384]{2,1,0:T(8,128)(2,1)S(1)}, f32[2,2,512,384]{3,2,1,0:T(8,128)S(1)}, bf16[2,3,2,1024,128]...) custom-call(s32[1]{0:T(128)S(6)} %copy.32.counts_ref, ...), custom_call_target="tpu_custom_call" | custom-call | flops 16307453952 | bytes 15728640 | tf_op jit(solution)/shard_map/patchwise/pallas_call | solution.py:1171
  87.9 0.3 collective-permute-start.6
  88.2 0.0 copy-done.5
  88.2 0.0 copy-done.7
  88.2 0.0 copy-start.3
  88.2 39.6 %attend_back_far.1 = (f32[2,3,1024,128]{3,2,1,0:T(8,128)S(1)}, bf16[2,3,1024,128]{3,2,1,0:T(8,128)(2,1)S(1)}, bf16[2,3,1024,128]{3,2,1,0:T(8,128)(2,1)S(1)}, bf1...) custom-call(bf16[2,3,2,1024,128]{4,3,2,1,0:T(8,128)(2,1)S(1)} %get-tuple-element.72.refs_0_,, ...), custom_call_target="tpu_custom_call" | custom-call | flops 16106127360 | tf_op jit(solution)/shard_map/attend_back_far/pallas_call | solution.py:1255
  127.9 0.0 collective-permute-done.6.got_ref
  127.9 0.0 copy-done.3
  127.9 5.7 %project_back_far.1 = (bf16[2,2,512,384]{3,2,1,0:T(8,128)(2,1)S(1)}, f32[384,768]{1,0:T(8,128)S(1)}, bf16[4,512,384]{2,1,0:T(8,128)(2,1)}) custom-call(bf16[2,3,1024,128]{3,2,1,0:T(8,128)(2,1)S(1)} %get-tuple-element.80.dk_ref, bf16[2,3,1024,128]{3,2,1,0:T(8,128)(2,1)S(1)} %get-tuple-element.81.dv_ref, bf16[2,2,512,384]{3,2,1,0:T(8,128)(2,1)S(1)} %bitcast.32, ...), custom_call_target="tpu_custom_call" | custom-call | flops 2415919104 | bytes 6291456 | tf_op jit(solution)/shard_map/project_back_far/pallas_call | solution.py:1274
  133.7 1.3 collective-permute-start.7
  135.0 37.4 %attend_back_near.1 = (bf16[2,3,1024,128]{3,2,1,0:T(8,128)(2,1)S(1)}, bf16[2,3,1024,128]{3,2,1,0:T(8,128)(2,1)S(1)}, bf16[2,3,1024,128]{3,2,1,0:T(8,128)(2,1)S(1...) custom-call(bf16[2,3,2,1024,128]{4,3,2,1,0:T(8,128)(2,1)S(1)} %get-tuple-element.72.refs_0_, ...), custom_call_target="tpu_custom_call" | custom-call | flops 16106127360 | tf_op jit(solution)/shard_map/attend_back_near/pallas_call | solution.py:1255
  172.3 5.1 %weight_back.1 = (bf16[9,384,128]{2,1,0:T(8,128)(2,1)S(1)}, f32[384,1536]{1,0:T(8,128)}, f32[1536,384]{1,0:T(8,128)}, f32[384,384]{1,0:T(8,128)}) custom-call(bf16[2,3,1024,128]{3,2,1,0:T(8,128)(2,1)S(1)} %get-tuple-element.89.refs_0_.refs_6_, bf16[2,3,1024,128]{3,2,1,0:T(8,128)(2,1)S(1)} %get-tuple-element.90.refs_1_.refs_7_, ...), custom_call_target="tpu_custom_call" | custom-call | flops 1811939328 | bytes 6291456 | tf_op jit(solution)/shard_map/weight_back/pallas_call | solution.py:1295
  177.4 0.0 collective-permute-done.7.refs_10_
  177.4 35.7 %tail.1 = (bf16[2,512,384]{2,1,0:T(8,128)(2,1)S(1)}, bf16[2,512,384]{2,1,0:T(8,128)(2,1)S(1)}, bf16[2,1792,128]{2,1,0:T(8,128)(2,1)S(1)}, bf16[2,16,16,128]{3,2,...) custom-call(bf16[2,1728,128]{2,1,0:T(8,128)(2,1)S(1)} %bitcast.33, ...), custom_call_target="tpu_custom_call" | custom-call | flops 1811939328 | tf_op jit(solution)/shard_map/tail/pallas_call | solution.py:1315
  213.2 4.7 %final.1 = (bf16[4,512,384]{2,1,0:T(8,128)(2,1)}, f32[16,384]{1,0:T(8,128)}, f32[384,2304]{1,0:T(8,128)}, f32[2304]{0:T(1024)}, f32[384,1152]{1,0:T(8,128)}) custom-call(bf16[512,128]{1,0:T(8,128)(2,1)S(1)} %bitcast.35, bf16[16,384]{1,0:T(8,128)(2,1)S(1)} %copy-done.8, bf16[384,2304]{1,0:T(8,128)(2,1)S(1)} %copy-done.1, ...), custom_call_target="tpu_custom_call" | custom-call | flops 905969664 | bytes 5308416 | tf_op jit(solution)/shard_map/final/pallas_call | solution.py:1375
  (1 shorter events, 0.0 us)
Async XLA Ops:
  0.7 3.2 %copy-start.13 = (bf16[4,1,512,384]{3,2,1,0:T(8,128)(2,1)S(1)}, bf16[4,1,512,384]{3,2,1,0:T(8,128)(2,1)}, u32[]{:S(2)}) copy-start(bf16[4,1,512,384]{3,2,1,0:T(8,128)(2,1)} %param.11) | copy-start | bytes 4718596
  3.2 5.3 %collective-permute-start.2 = (bf16[2,512,384]{2,1,0:T(8,128)(2,1)}, bf16[2,512,384]{2,1,0:T(8,128)(2,1)S(1)}, u32[]{:S(2)}, u32[]{:S(2)}) collective-permute-start(bf16[2,512,384]{2,1,0:T(8,128)(2,1)} %get-tuple-element.130), channel_id=1, source_target_pairs={{0,1},{1,0},{2,3},{3,2},{4,5},{5,4},{6,7},{7,6},{8,9},{9,8},{10,11... | collective-permute-start | bytes 2359304 | tf_op jit(solution)/shard_map/ppermute | solution.py:1077
  3.9 3.7 %copy-start.15 = (bf16[2304]{0:T(1024)(128)(2,1)S(1)}, bf16[2304]{0:T(1024)(128)(2,1)}, u32[]{:S(2)}) copy-start(bf16[2304]{0:T(1024)(128)(2,1)} %param.17) | copy-start | bytes 13828
  3.9 4.4 %copy-start.14 = (bf16[4,1,512,384]{3,2,1,0:T(8,128)(2,1)S(1)}, bf16[4,1,512,384]{3,2,1,0:T(8,128)(2,1)}, u32[]{:S(2)}) copy-start(bf16[4,1,512,384]{3,2,1,0:T(8,128)(2,1)} %param.12) | copy-start | bytes 4718596
  4.0 25.1 %collective-permute-start.3 = (bf16[1,512,384]{2,1,0:T(8,128)(2,1)S(1)}, bf16[1,512,384]{2,1,0:T(8,128)(2,1)S(1)}, u32[]{:S(2)}, u32[]{:S(2)}) collective-permute-start(bf16[1,512,384]{2,1,0:T(8,128)(2,1)S(1)} %get-tuple-element.127), channel_id=1, source_target_pairs={{0,2},{1,3},{2,0},{3,1},{4,6},{5,7},{6,4},{7,5},{8,10},{9,11},{10,... | collective-permute-start | bytes 1179656 | tf_op jit(solution)/shard_map/ppermute | solution.py:1077
  5.3 23.8 %collective-permute-start.4 = (bf16[1,512,384]{2,1,0:T(8,128)(2,1)S(1)}, bf16[1,512,384]{2,1,0:T(8,128)(2,1)S(1)}, u32[]{:S(2)}, u32[]{:S(2)}) collective-permute-start(bf16[1,512,384]{2,1,0:T(8,128)(2,1)S(1)} %get-tuple-element.126), channel_id=1, source_target_pairs={{0,3},{1,2},{2,1},{3,0},{4,7},{5,6},{6,5},{7,4},{8,11},{9,10},{10,... | collective-permute-start | bytes 1179656 | tf_op jit(solution)/shard_map/ppermute | solution.py:1077
  5.8 33.4 %collective-permute-start = (bf16[1,512,384]{2,1,0:T(8,128)(2,1)S(1)}, bf16[1,512,384]{2,1,0:T(8,128)(2,1)S(1)}, u32[]{:S(2)}, u32[]{:S(2)}) collective-permute-start(bf16[1,512,384]{2,1,0:T(8,128)(2,1)S(1)} %get-tuple-element.129), channel_id=1, source_target_pairs={{0,2},{1,3},{2,0},{3,1},{4,6},{5,7},{6,4},{7,5},{8,10},{9,11},{10,... | collective-permute-start | bytes 1179656 | tf_op jit(solution)/shard_map/ppermute | solution.py:1077
  7.0 33.2 %collective-permute-start.1 = (bf16[1,512,384]{2,1,0:T(8,128)(2,1)S(1)}, bf16[1,512,384]{2,1,0:T(8,128)(2,1)S(1)}, u32[]{:S(2)}, u32[]{:S(2)}) collective-permute-start(bf16[1,512,384]{2,1,0:T(8,128)(2,1)S(1)} %get-tuple-element.128), channel_id=1, source_target_pairs={{0,3},{1,2},{2,1},{3,0},{4,7},{5,6},{6,5},{7,4},{8,11},{9,10},{10,... | collective-permute-start | bytes 1179656 | tf_op jit(solution)/shard_map/ppermute | solution.py:1077
  8.3 1.2 copy-start
  8.3 1.7 copy-start.1
  8.3 1.7 copy-start.8
  8.3 1.7 copy-start.9
  8.5 45.1 %collective-permute-start.5 = (bf16[2,512,384]{2,1,0:T(8,128)(2,1)S(1)}, bf16[2,512,384]{2,1,0:T(8,128)(2,1)S(1)}, u32[]{:S(2)}, u32[]{:S(2)}) collective-permute-start(bf16[2,512,384]{2,1,0:T(8,128)(2,1)S(1)} %get-tuple-element.124), channel_id=1, source_target_pairs={{0,1},{1,0},{2,3},{3,2},{4,5},{5,4},{6,7},{7,6},{8,9},{9,8},{10,11... | collective-permute-start | bytes 2359304 | tf_op jit(solution)/shard_map/ppermute | solution.py:1077
  40.2 13.4 %copy-start.10 = (bf16[384,1536]{1,0:T(8,128)(2,1)S(1)}, bf16[384,1536]{1,0:T(8,128)(2,1)}, u32[]{:S(2)}) copy-start(bf16[384,1536]{1,0:T(8,128)(2,1)} %fc1_w.1) | copy-start | bytes 3538948
  40.2 13.4 %copy-start.11 = (bf16[1536,384]{1,0:T(8,128)(2,1)S(1)}, bf16[1536,384]{1,0:T(8,128)(2,1)}, u32[]{:S(2)}) copy-start(bf16[1536,384]{1,0:T(8,128)(2,1)} %fc2_w.1) | copy-start | bytes 3538948
  40.2 13.4 %copy-start.12 = (bf16[384,384]{1,0:T(8,128)(2,1)S(1)}, bf16[384,384]{1,0:T(8,128)(2,1)}, u32[]{:S(2)}) copy-start(bf16[384,384]{1,0:T(8,128)(2,1)} %out_w.1) | copy-start | bytes 884740
  50.2 1.1 copy-start.2
  51.3 1.1 copy-start.4
  52.5 1.1 copy-start.6
  53.6 34.6 %copy-start.5 = (bf16[2,3,1024,128]{3,2,1,0:T(8,128)(2,1)S(1)}, bf16[2,3,1024,128]{3,2,1,0:T(8,128)(2,1)}, u32[]{:S(2)}) copy-start(bf16[2,3,1024,128]{3,2,1,0:T(8,128)(2,1)} %copy-done.4) | copy-start | bytes 4718596
  53.7 34.6 %copy-start.7 = (bf16[2,3,1024,128]{3,2,1,0:T(8,128)(2,1)S(1)}, bf16[2,3,1024,128]{3,2,1,0:T(8,128)(2,1)}, u32[]{:S(2)}) copy-start(bf16[2,3,1024,128]{3,2,1,0:T(8,128)(2,1)} %copy-done.6) | copy-start | bytes 4718596
  87.9 40.0 %collective-permute-start.6 = (bf16[2,512,384]{2,1,0:T(8,128)(2,1)S(1)}, bf16[2,512,384]{2,1,0:T(8,128)(2,1)S(1)}, u32[]{:S(2)}, u32[]{:S(2)}) collective-permute-start(bf16[2,512,384]{2,1,0:T(8,128)(2,1)S(1)} %get-tuple-element.84), channel_id=1, source_target_pairs={{0,1},{1,0},{2,3},{3,2},{4,5},{5,4},{6,7},{7,6},{8,9},{9,8},{10,11... | collective-permute-start | bytes 2359304 | tf_op jit(solution)/shard_map/ppermute | solution.py:1077
  88.2 39.7 %copy-start.3 = (bf16[2,1024,384]{2,1,0:T(8,128)(2,1)S(1)}, bf16[2,1024,384]{2,1,0:T(8,128)(2,1)}, u32[]{:S(2)}) copy-start(bf16[2,1024,384]{2,1,0:T(8,128)(2,1)} %copy-done.2) | copy-start | bytes 4718596
  133.7 43.8 %collective-permute-start.7 = (bf16[2,2,512,384]{3,2,1,0:T(8,128)(2,1)S(1)}, bf16[2,2,512,384]{3,2,1,0:T(8,128)(2,1)S(1)}, u32[]{:S(2)}, u32[]{:S(2)}) collective-permute-start(bf16[2,2,512,384]{3,2,1,0:T(8,128)(2,1)S(1)} %get-tuple-element.98), channel_id=1, source_target_pairs={{0,2},{1,3},{2,0},{3,1},{4,6},{5,7},{6,4},{7,5},{8,10},{9,11},{10,... | collective-permute-start | bytes 4718600 | tf_op jit(solution)/shard_map/ppermute | solution.py:1077
